TPU v7x, 512 devices: a whole 4x8x8 slice. The times are simulated.
512 devices in a mesh: rep: 64 (over z, x, core), head: 8 (over y).
Axes of the slice: x: 4, y: 8, z: 8, core: 2. Of those that a mesh axis runs over, the one named last changes fastest.
Arguments:
- states: float32 [128, 32, 128, 128], P('rep', 'head'), may hold values from -4 to 4
- conv_states: bfloat16 [128, 3, 3, 4096], P('rep', None, None, 'head'), may hold values from -6 to 6
- projected: bfloat16 [6, 128, 3, 4096], P(None, 'rep', None, 'head'), may hold values from -6 to 6
- conv_weight: float32 [4, 3, 4096], P(None, None, 'head'), may hold values from -3 to 3
- decay_input: float32 [6, 128, 4096], P(None, 'rep', 'head'), may hold values from -6 to 6
- decay_rate: float32 [32], P('head'), may hold values from 0.05 to 2
- beta_logit: float32 [6, 128, 32], P(None, 'rep', 'head'), may hold values from -6 to 6
- out_gate: bfloat16 [6, 128, 4096], P(None, 'rep', 'head'), may hold values from -6 to 6
- norm_gain: float32 [128], replicated, may hold values from 0.25 to 1.75
- out_weight: bfloat16 [4096, 2304], P('head'), may hold values from -0.125 to 0.125
- destinations: int32 [6, 128], replicated, may hold values from 0 to 127, as said below
- live_counts: int32 [6, 64], P(None, 'rep'), may hold values from 1 to 2
Outputs:
- layer_out: bfloat16 [6, 128, 2304], P(None, 'rep', 'head')
- states_out: float32 [128, 32, 128, 128], P('rep', 'head')
- conv_out: bfloat16 [128, 3, 3, 4096], P('rep', None, None, 'head')
Inputs may be any that keep to these rules, and one draw needn't show every extreme that they name: For each step t, destinations[t] is a permutation of the 128 slots; slot g belongs to replica group g // 2. In every step, the number of slots g of each group with destinations[t, g] != g is exactly 1.
All inputs are finite; a program needn't handle non-finite values.
Results may differ from a plain program's by a relative error of at most 0.015.
Values may be sent and summed in bfloat16 or wider, within the bound.
A program may use at most 128 MiB of HBM per device.

v0:
```python
import jax
import jax.numpy as jnp
from jax import lax
from jax.sharding import PartitionSpec as P

STEPS = 6


EPSILON = 1e-06


def unit_rows(vectors):
    return vectors / jnp.sqrt(jnp.sum(vectors * vectors, axis=-1, keepdims=True) + EPSILON)


def move_every(memory, history, targets):
    spread_memory, spread_history = (
        lax.all_to_all(memory, "rep", split_axis=2, concat_axis=0, tiled=True),
        lax.all_to_all(history.astype(jnp.float32), "rep", split_axis=2, concat_axis=0, tiled=True),
    )
    slot_total = spread_memory.shape[0]
    source = (
        jnp.zeros((slot_total,), jnp.int32).at[targets].set(jnp.arange(slot_total, dtype=jnp.int32))
    )
    back_memory, back_history = (
        lax.all_to_all(spread_memory[source], "rep", split_axis=0, concat_axis=2, tiled=True),
        lax.all_to_all(spread_history[source], "rep", split_axis=0, concat_axis=2, tiled=True),
    )
    return (back_memory, back_history.astype(jnp.bfloat16))


def layer_step(
    memory,
    history,
    proj_rows,
    decay_rows,
    gate_rows,
    beta_rows,
    alive,
    filters,
    decay_rate,
    norm_gain,
    out_weight,
):
    row_count, head_count, key_dim = (memory.shape[0], memory.shape[1], memory.shape[2])
    channels = filters.shape[1]
    tap_count = filters.shape[0]
    window = jnp.concatenate(
        [
            history.astype(jnp.float32),
            proj_rows.reshape(row_count, 1, channels).astype(jnp.float32),
        ],
        axis=1,
    )
    summed = window[:, 0] * filters[0]
    for tap_id in range(1, tap_count):
        summed = summed + window[:, tap_id] * filters[tap_id]
    activated = jax.nn.silu(summed).reshape(row_count, 3, head_count, key_dim)
    shifted = window[:, 1:].astype(jnp.bfloat16)
    query = unit_rows(activated[:, 0])
    key_vec = unit_rows(activated[:, 1])
    value_vec = activated[:, 2]
    retain = jnp.exp(
        -decay_rate[None, :, None]
        * jax.nn.softplus(decay_rows.reshape(row_count, head_count, key_dim))
    )
    strength = jax.nn.sigmoid(beta_rows)
    decayed = retain[..., None] * memory
    recalled = jnp.sum(key_vec[..., None] * decayed, axis=2)
    updated = (
        decayed
        + strength[..., None, None] * key_vec[..., None] * (value_vec - recalled)[:, :, None, :]
    )
    readout = jnp.sum(query[..., None] * updated, axis=2) * key_dim ** (-0.5)
    memory = jnp.where(alive[:, None, None, None], updated, memory)
    history = jnp.where(alive[:, None, None], shifted, history)
    scaling = lax.rsqrt(jnp.mean(readout * readout, axis=-1, keepdims=True) + EPSILON)
    gates = jax.nn.sigmoid(gate_rows.astype(jnp.float32).reshape(row_count, head_count, key_dim))
    gated = readout * scaling * norm_gain * gates
    gated = (
        jnp.where(alive[:, None, None], gated, jnp.zeros_like(gated))
        .astype(jnp.bfloat16)
        .reshape(row_count, head_count * key_dim)
    )
    partial_sum = jnp.dot(gated, out_weight, preferred_element_type=jnp.float32)
    out_rows = lax.psum_scatter(partial_sum, "head", scatter_dimension=1, tiled=True).astype(
        jnp.bfloat16
    )
    return (memory, history, out_rows)


def local(
    states,
    conv_states,
    projected,
    conv_weight,
    decay_input,
    decay_rate,
    beta_logit,
    out_gate,
    norm_gain,
    out_weight,
    destinations,
    live_counts,
):
    row_count = states.shape[0]
    channels = 3 * conv_states.shape[3]
    tap_count = conv_weight.shape[0]
    filters = conv_weight.reshape(tap_count, channels)
    history = conv_states.reshape(row_count, tap_count - 1, channels)
    memory = states
    slot_ids = jnp.arange(row_count, dtype=jnp.int32)
    results = []
    for step_id in range(STEPS):
        targets = destinations[step_id]
        memory, history = move_every(memory, history, targets)
        alive = slot_ids < live_counts[step_id, 0]
        memory, history, out_rows = layer_step(
            memory,
            history,
            projected[step_id],
            decay_input[step_id],
            out_gate[step_id],
            beta_logit[step_id],
            alive,
            filters,
            decay_rate,
            norm_gain,
            out_weight,
        )
        results.append(out_rows)
    return (jnp.stack(results), memory, history.reshape(conv_states.shape))


def solution(mesh):
    placed = (
        P("rep", "head", None, None),
        P("rep", None, None, "head"),
        P(None, "rep", None, "head"),
        P(None, None, "head"),
        P(None, "rep", "head"),
        P("head"),
        P(None, "rep", "head"),
        P(None, "rep", "head"),
        P(),
        P("head", None),
        P(),
        P(None, "rep"),
    )
    return jax.shard_map(
        local,
        mesh=mesh,
        in_specs=placed,
        out_specs=(
            P(None, "rep", "head"),
            P("rep", "head", None, None),
            P("rep", None, None, "head"),
        ),
        check_vma=False,
    )
```

profile of v0, /device:TPU:1, one launch (start us, length us, event | category | flops | bytes accessed | tf_op | source)
XLA Modules:
  0.0 901.9 jit_solution(8551852616792293892)
XLA Ops:
  9.9 14.8 %all-to-all-start = ((bf16[2,3,1536]{1,0,2:T(2,128)(2,1)}), bf16[2,3,1536]{1,0,2:T(2,128)(2,1)S(1)}, u32[]{:S(2)}, u32[]{:S(2)}) async-start(bf16[2,3,1536]{1,0,2:T(2,128)(2,1)} %copy.847), calls=%async_computation | async-start | bytes 1572864 | tf_op jit(solution)/shard_map/all_to_all | solution.py:19
  58.2 10.3 %all-to-all-start.1 = ((bf16[128,3,24]{2,1,0:T(4,128)(2,1)}), bf16[128,3,24]{2,1,0:T(4,128)(2,1)S(1)}, u32[]{:S(2)}, u32[]{:S(2)}) async-start(bf16[128,3,24]{2,1,0:T(4,128)(2,1)} %gather_fusion), calls=%async_computation.1 | async-start | bytes 262144 | tf_op jit(solution)/shard_map/all_to_all | solution.py:27
  69.2 10.4 %all-to-all-done.1 = bf16[128,3,24]{2,1,0:T(4,128)(2,1)S(1)} async-done(((bf16[128,3,24]{2,1,0:T(4,128)(2,1)}), bf16[128,3,24]{2,1,0:T(4,128)(2,1)S(1)}, u32[]{:S(2)}, u32[]{:S(2)}) %all-to-all-start.1) | async-done | bytes 18464 | tf_op jit(solution)/shard_map/all_to_all | solution.py:27
  87.5 21.7 %all-to-all-done.4 = bf16[2,3,1536]{1,0,2:T(2,128)(2,1)S(1)} async-done(((bf16[2,3,1536]{1,0,2:T(2,128)(2,1)}), bf16[2,3,1536]{1,0,2:T(2,128)(2,1)S(1)}, u32[]{:S(2)}, u32[]{:S(2)}) %all-to-all-start.4) | async-done | bytes 18464 | tf_op jit(solution)/shard_map/all_to_all | solution.py:19
  119.3 10.5 %all-to-all-done.5 = bf16[128,3,24]{2,1,0:T(4,128)(2,1)S(1)} async-done(((bf16[128,3,24]{2,1,0:T(4,128)(2,1)}), bf16[128,3,24]{2,1,0:T(4,128)(2,1)S(1)}, u32[]{:S(2)}, u32[]{:S(2)}) %all-to-all-start.5) | async-done | bytes 18464 | tf_op jit(solution)/shard_map/all_to_all | solution.py:27
  138.2 21.8 %all-to-all-done.8 = bf16[2,3,1536]{1,0,2:T(2,128)(2,1)S(1)} async-done(((bf16[2,3,1536]{1,0,2:T(2,128)(2,1)}), bf16[2,3,1536]{1,0,2:T(2,128)(2,1)S(1)}, u32[]{:S(2)}, u32[]{:S(2)}) %all-to-all-start.8) | async-done | bytes 18464 | tf_op jit(solution)/shard_map/all_to_all | solution.py:19
  185.2 10.3 %all-to-all-start.12 = ((bf16[2,3,1536]{1,0,2:T(2,128)(2,1)}), bf16[2,3,1536]{1,0,2:T(2,128)(2,1)S(1)}, u32[]{:S(2)}, u32[]{:S(2)}) async-start(bf16[2,3,1536]{1,0,2:T(2,128)(2,1)} %copy.929), calls=%async_computation.12 | async-start | bytes 1572864 | tf_op jit(solution)/shard_map/all_to_all | solution.py:19
  197.4 20.9 %all-to-all-done.12 = bf16[2,3,1536]{1,0,2:T(2,128)(2,1)S(1)} async-done(((bf16[2,3,1536]{1,0,2:T(2,128)(2,1)}), bf16[2,3,1536]{1,0,2:T(2,128)(2,1)S(1)}, u32[]{:S(2)}, u32[]{:S(2)}) %all-to-all-start.12) | async-done | bytes 18464 | tf_op jit(solution)/shard_map/all_to_all | solution.py:19
  221.8 6.2 all-to-all-start.13
  229.9 9.2 %all-to-all-done.13 = bf16[128,3,24]{2,1,0:T(4,128)(2,1)S(1)} async-done(((bf16[128,3,24]{2,1,0:T(4,128)(2,1)}), bf16[128,3,24]{2,1,0:T(4,128)(2,1)S(1)}, u32[]{:S(2)}, u32[]{:S(2)}) %all-to-all-start.13) | async-done | bytes 18464 | tf_op jit(solution)/shard_map/all_to_all | solution.py:27
  248.3 21.1 %all-to-all-done.16 = bf16[2,3,1536]{1,0,2:T(2,128)(2,1)S(1)} async-done(((bf16[2,3,1536]{1,0,2:T(2,128)(2,1)}), bf16[2,3,1536]{1,0,2:T(2,128)(2,1)S(1)}, u32[]{:S(2)}, u32[]{:S(2)}) %all-to-all-start.16) | async-done | bytes 18464 | tf_op jit(solution)/shard_map/all_to_all | solution.py:19
  279.1 11.0 %all-to-all-done.17 = bf16[128,3,24]{2,1,0:T(4,128)(2,1)S(1)} async-done(((bf16[128,3,24]{2,1,0:T(4,128)(2,1)}), bf16[128,3,24]{2,1,0:T(4,128)(2,1)S(1)}, u32[]{:S(2)}, u32[]{:S(2)}) %all-to-all-start.17) | async-done | bytes 18464 | tf_op jit(solution)/shard_map/all_to_all | solution.py:27
  304.4 8.0 all-to-all-done.2
  325.8 15.8 %all-to-all-done.20 = bf16[2,3,1536]{1,0,2:T(2,128)(2,1)S(1)} async-done(((bf16[2,3,1536]{1,0,2:T(2,128)(2,1)}), bf16[2,3,1536]{1,0,2:T(2,128)(2,1)S(1)}, u32[]{:S(2)}, u32[]{:S(2)}) %all-to-all-start.20) | async-done | bytes 18464 | tf_op jit(solution)/shard_map/all_to_all | solution.py:19
  341.7 6.4 all-to-all-start.3
  377.5 10.3 %all-to-all-start.21 = ((bf16[128,3,24]{2,1,0:T(4,128)(2,1)}), bf16[128,3,24]{2,1,0:T(4,128)(2,1)S(1)}, u32[]{:S(2)}, u32[]{:S(2)}) async-start(bf16[128,3,24]{2,1,0:T(4,128)(2,1)} %gather_fusion.10), calls=%async_computation.21 | async-start | bytes 262144 | tf_op jit(solution)/shard_map/all_to_all | solution.py:27
  410.2 11.6 %all-to-all-done.6 = f32[2,4,128,128]{3,1,0,2:T(4,128)S(1)} async-done(((f32[2,4,128,128]{3,1,0,2:T(4,128)}), f32[2,4,128,128]{3,1,0,2:T(4,128)S(1)}, u32[]{:S(2)}, u32[]{:S(2)}) %all-to-all-start.6) | async-done | bytes 524320 | tf_op jit(solution)/shard_map/all_to_all | solution.py:18
  437.4 10.6 %all-to-all-done.7 = f32[128,4,2,128]{3,1,2,0:T(4,128)} async-done(((f32[128,4,2,128]{3,1,2,0:T(4,128)}), f32[128,4,2,128]{3,1,2,0:T(4,128)}, u32[]{:S(2)}, u32[]{:S(2)}) %all-to-all-start.7) | async-done | bytes 524320 | tf_op jit(solution)/shard_map/all_to_all | solution.py:26
  483.7 7.9 all-to-all-start.11
  497.6 11.7 %all-to-all-done.11 = f32[128,4,2,128]{3,1,2,0:T(4,128)} async-done(((f32[128,4,2,128]{3,1,2,0:T(4,128)}), f32[128,4,2,128]{3,1,2,0:T(4,128)}, u32[]{:S(2)}, u32[]{:S(2)}) %all-to-all-start.11) | async-done | bytes 524320 | tf_op jit(solution)/shard_map/all_to_all | solution.py:26
  516.3 6.3 all-to-all-start.14
  532.0 8.3 all-to-all-done.14
  570.2 21.4 %reduce-scatter.19.cloned.1.call-done = f32[288,2]{1,0:T(8,128)} async-done(((f32[2304,2]{1,0:T(8,128)}), f32[288,2]{1,0:T(8,128)}) %reduce-scatter.19.cloned.1.call-update) | async-done | bytes 2320
  601.2 15.6 %all-to-all-start.18 = ((f32[2,4,128,128]{3,1,0,2:T(4,128)}), f32[2,4,128,128]{3,1,0,2:T(4,128)}, u32[]{:S(2)}, u32[]{:S(2)}) async-start(f32[2,4,128,128]{3,1,0,2:T(4,128)} %copy.972), calls=%async_computation.18 | async-start | bytes 1048576 | tf_op jit(solution)/shard_map/all_to_all | solution.py:18
  619.3 36.7 %reduce-scatter.21.cloned.1.call-done = f32[288,2]{1,0:T(8,128)} async-done(((f32[2304,2]{1,0:T(8,128)}), f32[288,2]{1,0:T(8,128)}) %reduce-scatter.21.cloned.1.call-update) | async-done | bytes 2320
  664.1 15.5 %all-to-all-start.19 = ((f32[128,4,2,128]{3,1,2,0:T(4,128)}), f32[128,4,2,128]{3,1,2,0:T(4,128)}, u32[]{:S(2)}, u32[]{:S(2)}) async-start(f32[128,4,2,128]{3,1,2,0:T(4,128)} %gather_fusion.9), calls=%async_computation.19 | async-start | bytes 1048576 | tf_op jit(solution)/shard_map/all_to_all | solution.py:26
  681.9 36.8 %reduce-scatter.23.cloned.1.call-done = f32[288,2]{1,0:T(8,128)} async-done(((f32[2304,2]{1,0:T(8,128)}), f32[288,2]{1,0:T(8,128)}) %reduce-scatter.23.cloned.1.call-update) | async-done | bytes 2320
  728.4 15.5 %all-to-all-start.22 = ((f32[2,4,128,128]{3,1,0,2:T(4,128)}), f32[2,4,128,128]{3,1,0,2:T(4,128)}, u32[]{:S(2)}, u32[]{:S(2)}) async-start(f32[2,4,128,128]{3,1,0,2:T(4,128)} %copy.1000), calls=%async_computation.22 | async-start | bytes 1048576 | tf_op jit(solution)/shard_map/all_to_all | solution.py:18
  746.1 36.8 %reduce-scatter.25.cloned.1.call-done = f32[288,2]{1,0:T(8,128)} async-done(((f32[2304,2]{1,0:T(8,128)}), f32[288,2]{1,0:T(8,128)}) %reduce-scatter.25.cloned.1.call-update) | async-done | bytes 2320
  790.7 15.2 %all-to-all-start.23 = ((f32[128,4,2,128]{3,1,2,0:T(4,128)}), f32[128,4,2,128]{3,1,2,0:T(4,128)S(1)}, u32[]{:S(2)}, u32[]{:S(2)}) async-start(f32[128,4,2,128]{3,1,2,0:T(4,128)} %gather_fusion.11), calls=%async_computation.23 | async-start | bytes 1048576 | tf_op jit(solution)/shard_map/all_to_all | solution.py:26
  808.3 36.3 %reduce-scatter.27.cloned.1.call-done = f32[288,2]{1,0:T(8,128)} async-done(((f32[2304,2]{1,0:T(8,128)}), f32[288,2]{1,0:T(8,128)}) %reduce-scatter.27.cloned.1.call-update) | async-done | bytes 2320
  853.8 39.4 %reduce-scatter.29.cloned.1.call-done = f32[288,2]{1,0:T(8,128)} async-done(((f32[2304,2]{1,0:T(8,128)}), f32[288,2]{1,0:T(8,128)}) %reduce-scatter.29.cloned.1.call-update) | async-done | bytes 2320
  (480 shorter events, 351.3 us)
Async XLA Ops:
  7.2 542.8 %copy-start = (bf16[512,2304]{1,0:T(8,128)(2,1)S(1)}, bf16[512,2304]{1,0:T(8,128)(2,1)}, u32[]{:S(2)}) copy-start(bf16[512,2304]{1,0:T(8,128)(2,1)} %param.21) | copy-start | bytes 7077892
  9.9 44.9 %all-to-all-start = ((bf16[2,3,1536]{1,0,2:T(2,128)(2,1)}), bf16[2,3,1536]{1,0,2:T(2,128)(2,1)S(1)}, u32[]{:S(2)}, u32[]{:S(2)}) async-start(bf16[2,3,1536]{1,0,2:T(2,128)(2,1)} %copy.847), calls=%async_computation | async-start | bytes 1572864 | tf_op jit(solution)/shard_map/all_to_all | solution.py:19
  58.2 21.4 %all-to-all-start.1 = ((bf16[128,3,24]{2,1,0:T(4,128)(2,1)}), bf16[128,3,24]{2,1,0:T(4,128)(2,1)S(1)}, u32[]{:S(2)}, u32[]{:S(2)}) async-start(bf16[128,3,24]{2,1,0:T(4,128)(2,1)} %gather_fusion), calls=%async_computation.1 | async-start | bytes 262144 | tf_op jit(solution)/shard_map/all_to_all | solution.py:27
  81.7 27.5 %all-to-all-start.4 = ((bf16[2,3,1536]{1,0,2:T(2,128)(2,1)}), bf16[2,3,1536]{1,0,2:T(2,128)(2,1)S(1)}, u32[]{:S(2)}, u32[]{:S(2)}) async-start(bf16[2,3,1536]{1,0,2:T(2,128)(2,1)} %copy.873), calls=%async_computation.4 | async-start | bytes 1572864 | tf_op jit(solution)/shard_map/all_to_all | solution.py:19
  112.5 17.2 %all-to-all-start.5 = ((bf16[128,3,24]{2,1,0:T(4,128)(2,1)}), bf16[128,3,24]{2,1,0:T(4,128)(2,1)S(1)}, u32[]{:S(2)}, u32[]{:S(2)}) async-start(bf16[128,3,24]{2,1,0:T(4,128)(2,1)} %gather_fusion.2), calls=%async_computation.5 | async-start | bytes 262144 | tf_op jit(solution)/shard_map/all_to_all | solution.py:27
  131.9 28.1 %all-to-all-start.8 = ((bf16[2,3,1536]{1,0,2:T(2,128)(2,1)}), bf16[2,3,1536]{1,0,2:T(2,128)(2,1)S(1)}, u32[]{:S(2)}, u32[]{:S(2)}) async-start(bf16[2,3,1536]{1,0,2:T(2,128)(2,1)} %copy.901), calls=%async_computation.8 | async-start | bytes 1572864 | tf_op jit(solution)/shard_map/all_to_all | solution.py:19
  163.4 19.7 %all-to-all-start.9 = ((bf16[128,3,24]{2,1,0:T(4,128)(2,1)}), bf16[128,3,24]{2,1,0:T(4,128)(2,1)S(1)}, u32[]{:S(2)}, u32[]{:S(2)}) async-start(bf16[128,3,24]{2,1,0:T(4,128)(2,1)} %gather_fusion.4), calls=%async_computation.9 | async-start | bytes 262144 | tf_op jit(solution)/shard_map/all_to_all | solution.py:27
  175.5 213.9 %copy-start.7 = (f32[2,4,64,2]{0,2,3,1:T(8,128)}, f32[2,4,64,2]{0,2,3,1:T(8,128)S(1)}, u32[]{:S(2)}) copy-start(f32[2,4,64,2]{0,2,3,1:T(8,128)S(1)} %copy.860) | copy-start | bytes 12292
  185.2 33.1 %all-to-all-start.12 = ((bf16[2,3,1536]{1,0,2:T(2,128)(2,1)}), bf16[2,3,1536]{1,0,2:T(2,128)(2,1)S(1)}, u32[]{:S(2)}, u32[]{:S(2)}) async-start(bf16[2,3,1536]{1,0,2:T(2,128)(2,1)} %copy.929), calls=%async_computation.12 | async-start | bytes 1572864 | tf_op jit(solution)/shard_map/all_to_all | solution.py:19
  221.8 17.4 %all-to-all-start.13 = ((bf16[128,3,24]{2,1,0:T(4,128)(2,1)}), bf16[128,3,24]{2,1,0:T(4,128)(2,1)S(1)}, u32[]{:S(2)}, u32[]{:S(2)}) async-start(bf16[128,3,24]{2,1,0:T(4,128)(2,1)} %gather_fusion.6), calls=%async_computation.13 | async-start | bytes 262144 | tf_op jit(solution)/shard_map/all_to_all | solution.py:27
  241.9 27.5 %all-to-all-start.16 = ((bf16[2,3,1536]{1,0,2:T(2,128)(2,1)}), bf16[2,3,1536]{1,0,2:T(2,128)(2,1)S(1)}, u32[]{:S(2)}, u32[]{:S(2)}) async-start(bf16[2,3,1536]{1,0,2:T(2,128)(2,1)} %copy.957), calls=%async_computation.16 | async-start | bytes 1572864 | tf_op jit(solution)/shard_map/all_to_all | solution.py:19
  272.9 17.2 %all-to-all-start.17 = ((bf16[128,3,24]{2,1,0:T(4,128)(2,1)}), bf16[128,3,24]{2,1,0:T(4,128)(2,1)S(1)}, u32[]{:S(2)}, u32[]{:S(2)}) async-start(bf16[128,3,24]{2,1,0:T(4,128)(2,1)} %gather_fusion.8), calls=%async_computation.17 | async-start | bytes 262144 | tf_op jit(solution)/shard_map/all_to_all | solution.py:27
  290.1 22.3 %all-to-all-start.2 = ((f32[2,4,128,128]{3,1,0,2:T(4,128)}), f32[2,4,128,128]{3,1,0,2:T(4,128)S(1)}, u32[]{:S(2)}, u32[]{:S(2)}) async-start(f32[2,4,128,128]{3,1,0,2:T(4,128)} %copy.861), calls=%async_computation.2 | async-start | bytes 1048576 | tf_op jit(solution)/shard_map/all_to_all | solution.py:18
  313.2 28.5 %all-to-all-start.20 = ((bf16[2,3,1536]{1,0,2:T(2,128)(2,1)}), bf16[2,3,1536]{1,0,2:T(2,128)(2,1)S(1)}, u32[]{:S(2)}, u32[]{:S(2)}) async-start(bf16[2,3,1536]{1,0,2:T(2,128)(2,1)} %copy.985), calls=%async_computation.20 | async-start | bytes 1572864 | tf_op jit(solution)/shard_map/all_to_all | solution.py:19
  341.7 35.8 %all-to-all-start.3 = ((f32[128,4,2,128]{3,1,2,0:T(4,128)}), f32[128,4,2,128]{3,1,2,0:T(4,128)}, u32[]{:S(2)}, u32[]{:S(2)}) async-start(f32[128,4,2,128]{3,1,2,0:T(4,128)} %gather_fusion.1), calls=%async_computation.3 | async-start | bytes 1048576 | tf_op jit(solution)/shard_map/all_to_all | solution.py:26
  377.5 21.4 %all-to-all-start.21 = ((bf16[128,3,24]{2,1,0:T(4,128)(2,1)}), bf16[128,3,24]{2,1,0:T(4,128)(2,1)S(1)}, u32[]{:S(2)}, u32[]{:S(2)}) async-start(bf16[128,3,24]{2,1,0:T(4,128)(2,1)} %gather_fusion.10), calls=%async_computation.21 | async-start | bytes 262144 | tf_op jit(solution)/shard_map/all_to_all | solution.py:27
  398.9 22.9 %all-to-all-start.6 = ((f32[2,4,128,128]{3,1,0,2:T(4,128)}), f32[2,4,128,128]{3,1,0,2:T(4,128)S(1)}, u32[]{:S(2)}, u32[]{:S(2)}) async-start(f32[2,4,128,128]{3,1,0,2:T(4,128)} %copy.888), calls=%async_computation.6 | async-start | bytes 1048576 | tf_op jit(solution)/shard_map/all_to_all | solution.py:18
  424.4 23.6 %all-to-all-start.7 = ((f32[128,4,2,128]{3,1,2,0:T(4,128)}), f32[128,4,2,128]{3,1,2,0:T(4,128)}, u32[]{:S(2)}, u32[]{:S(2)}) async-start(f32[128,4,2,128]{3,1,2,0:T(4,128)} %gather_fusion.3), calls=%async_computation.7 | async-start | bytes 1048576 | tf_op jit(solution)/shard_map/all_to_all | solution.py:26
  454.6 23.6 %all-to-all-start.10 = ((f32[2,4,128,128]{3,1,0,2:T(4,128)}), f32[2,4,128,128]{3,1,0,2:T(4,128)}, u32[]{:S(2)}, u32[]{:S(2)}) async-start(f32[2,4,128,128]{3,1,0,2:T(4,128)} %copy.916), calls=%async_computation.10 | async-start | bytes 1048576 | tf_op jit(solution)/shard_map/all_to_all | solution.py:18
  483.7 25.6 %all-to-all-start.11 = ((f32[128,4,2,128]{3,1,2,0:T(4,128)}), f32[128,4,2,128]{3,1,2,0:T(4,128)}, u32[]{:S(2)}, u32[]{:S(2)}) async-start(f32[128,4,2,128]{3,1,2,0:T(4,128)} %gather_fusion.5), calls=%async_computation.11 | async-start | bytes 1048576 | tf_op jit(solution)/shard_map/all_to_all | solution.py:26
  516.3 24.0 %all-to-all-start.14 = ((f32[2,4,128,128]{3,1,0,2:T(4,128)}), f32[2,4,128,128]{3,1,0,2:T(4,128)}, u32[]{:S(2)}, u32[]{:S(2)}) async-start(f32[2,4,128,128]{3,1,0,2:T(4,128)} %copy.944), calls=%async_computation.14 | async-start | bytes 1048576 | tf_op jit(solution)/shard_map/all_to_all | solution.py:18
  544.0 51.8 %all-to-all-start.15 = ((f32[128,4,2,128]{3,1,2,0:T(4,128)}), f32[128,4,2,128]{3,1,2,0:T(4,128)}, u32[]{:S(2)}, u32[]{:S(2)}) async-start(f32[128,4,2,128]{3,1,2,0:T(4,128)} %gather_fusion.7), calls=%async_computation.15 | async-start | bytes 1048576 | tf_op jit(solution)/shard_map/all_to_all | solution.py:26
  549.9 41.6 %reduce-scatter.19.cloned.1.call-start = ((), (), s32[]{:S(2)}) async-start(), calls=%async_computation.30 | async-start | bytes 1327104
  601.2 59.2 %all-to-all-start.18 = ((f32[2,4,128,128]{3,1,0,2:T(4,128)}), f32[2,4,128,128]{3,1,0,2:T(4,128)}, u32[]{:S(2)}, u32[]{:S(2)}) async-start(f32[2,4,128,128]{3,1,0,2:T(4,128)} %copy.972), calls=%async_computation.18 | async-start | bytes 1048576 | tf_op jit(solution)/shard_map/all_to_all | solution.py:18
  616.9 39.1 %reduce-scatter.21.cloned.1.call-start = ((), (), s32[]{:S(2)}) async-start(), calls=%async_computation.31 | async-start | bytes 1327104
  664.1 58.9 %all-to-all-start.19 = ((f32[128,4,2,128]{3,1,2,0:T(4,128)}), f32[128,4,2,128]{3,1,2,0:T(4,128)}, u32[]{:S(2)}, u32[]{:S(2)}) async-start(f32[128,4,2,128]{3,1,2,0:T(4,128)} %gather_fusion.9), calls=%async_computation.19 | async-start | bytes 1048576 | tf_op jit(solution)/shard_map/all_to_all | solution.py:26
  679.7 39.0 %reduce-scatter.23.cloned.1.call-start = ((), (), s32[]{:S(2)}) async-start(), calls=%async_computation.32 | async-start | bytes 1327104
  728.4 58.7 %all-to-all-start.22 = ((f32[2,4,128,128]{3,1,0,2:T(4,128)}), f32[2,4,128,128]{3,1,0,2:T(4,128)}, u32[]{:S(2)}, u32[]{:S(2)}) async-start(f32[2,4,128,128]{3,1,0,2:T(4,128)} %copy.1000), calls=%async_computation.22 | async-start | bytes 1048576 | tf_op jit(solution)/shard_map/all_to_all | solution.py:18
  743.9 39.0 %reduce-scatter.25.cloned.1.call-start = ((), (), s32[]{:S(2)}) async-start(), calls=%async_computation.33 | async-start | bytes 1327104
  790.7 54.9 %all-to-all-start.23 = ((f32[128,4,2,128]{3,1,2,0:T(4,128)}), f32[128,4,2,128]{3,1,2,0:T(4,128)S(1)}, u32[]{:S(2)}, u32[]{:S(2)}) async-start(f32[128,4,2,128]{3,1,2,0:T(4,128)} %gather_fusion.11), calls=%async_computation.23 | async-start | bytes 1048576 | tf_op jit(solution)/shard_map/all_to_all | solution.py:26
  805.9 38.7 %reduce-scatter.27.cloned.1.call-start = ((), (), s32[]{:S(2)}) async-start(), calls=%async_computation.34 | async-start | bytes 1327104
  808.2 85.0 %reduce-scatter.29.cloned.1.call-start = ((), (), s32[]{:S(2)}) async-start(), calls=%async_computation.35 | async-start | bytes 1327104
  (67 other events, 2062.8 us)
Sparse Core Ops, SparseCore 0:
  553.6 37.9 reduce-scatter.18
  620.6 35.3 reduce-scatter.20
  683.3 35.3 reduce-scatter.22
  747.2 35.5 reduce-scatter.24
  809.3 35.3 reduce-scatter.26
  852.8 40.3 reduce-scatter.28
where the time goes:
time: 919 us; the launch traced here: 902 us
  waiting for transfers between devices  408 us (44%)
  starting transfers between devices  200 us (22%)
  local copies, waits for them, and re-layouts  173 us (19%)
  other arithmetic  91.2 us (10%)
  between operations  16.1 us (2%)
  matrix products  13.3 us (1%)
    unnamed x12, waiting for transfers between devices  207 us
    all_to_all x6, waiting for transfers between devices, move_every(): lax.all_to_all(history.astype(jnp.float32), 'rep', split_axis=2, concat_a...  101 us
    all_to_all x6, starting transfers between devices, move_every(): lax.all_to_all(spread_memory[source], 'rep', split_axis=0, concat_axis=2,...  56.9 us
    all_to_all x6, starting transfers between devices, move_every(): lax.all_to_all(memory, 'rep', split_axis=2, concat_axis=0, tiled=True)  53.2 us
    all_to_all x6, waiting for transfers between devices, move_every(): lax.all_to_all(spread_history[source], 'rep', split_axis=0, concat_axis=2...  46.5 us
    all_to_all x6, starting transfers between devices, move_every(): lax.all_to_all(spread_history[source], 'rep', split_axis=0, concat_axis=2...  45.1 us
    all_to_all x6, starting transfers between devices, move_every(): lax.all_to_all(history.astype(jnp.float32), 'rep', split_axis=2, concat_a...  44.9 us
    all_to_all x6, waiting for transfers between devices, move_every(): lax.all_to_all(memory, 'rep', split_axis=2, concat_axis=0, tiled=True)  30.5 us
  transfers between devices with their start and end apart: 30, of which 22 were waited for; matrix products, arithmetic and copies ran while one was open for 22% of the time, Pallas kernels for 0%

commit v1 on v0

v1 whole, which is shorter than its diff:
```python
import functools

import jax
import jax.numpy as jnp
from jax import lax
from jax.experimental import pallas as pl
from jax.experimental.pallas import tpu as pltpu
from jax.sharding import PartitionSpec as P

F32, BF16 = jnp.float32, jnp.bfloat16
STEPS, TAPS = 6, 4
HIST = TAPS - 1
GROUPS, HEADS, DK = 64, 4, 128
SLOTS = 2 * GROUPS
JG, JW = 16, 8
WIN = HIST + STEPS
ROW_X = 0
ROW_HI = WIN * 6
ROW_LO = ROW_HI + 2 * STEPS
ROW_MISC = ROW_LO + 2 * STEPS
ROWS = ROW_MISC + 2
CONV = 3 * HIST
BLOCKS = CONV + STEPS
EPS = 1e-6


def piece_of(m):
    return (m // 8) % HEADS, (m // 32) * 8 + m % 8


def holder(h, jg):
    return (jg // 8) * 32 + h * 8 + jg % 8


def iota(shape, dim):
    return lax.broadcasted_iota(jnp.int32, shape, dim)


def contract(a, b, da, db):
    return lax.dot_general(a, b, (((da,), (db,)), ((), ())), preferred_element_type=F32)


def halves(x):
    lead = x.astype(BF16)
    return lead, (x - lead.astype(F32)).astype(BF16)


def sigmoid(x):
    return 1.0 / (1.0 + jnp.exp(-x))


def softplus(x):
    return jnp.maximum(x, 0.0) + jnp.log1p(jnp.exp(-jnp.abs(x)))


def pack(states, conv, proj, decay, beta, live, s1, s2, f):
    for h in range(HEADS):
        cols = slice(h * DK, (h + 1) * DK)
        first, second = states[0, h].T, states[1, h].T
        for jg in range(JG):
            rows = slice(jg * JW, (jg + 1) * JW)
            s1[holder(h, jg)] = jnp.concatenate([first[rows], second[rows]], axis=0).astype(BF16)
        lane = iota((1, DK), 1)
        for slot in range(2):
            row = jnp.zeros((1, DK), F32)
            for t in range(STEPS):
                alive = jnp.where(live[t, 0] > slot, 1.0, 0.0)
                logit = beta[t, slot, h]
                row = jnp.where(lane == t * 8, alive, row)
                row = jnp.where((lane == t * 8 + 1) | (lane == t * 8 + 2), logit, row)
            lead, rest = halves(row)
            f[h, ROW_MISC + slot : ROW_MISC + slot + 1, :] = jnp.where(
                lane % 8 == 2, rest.astype(F32), lead.astype(F32)
            )
    for w in range(WIN):
        for slot in range(2):
            block = (conv[slot, w] if w < HIST else proj[w - HIST, slot]).astype(F32)
            at = ROW_X + (w * 2 + slot) * 3
            for h in range(HEADS):
                f[h, at : at + 3, :] = block[:, h * DK : (h + 1) * DK]
    for t in range(STEPS):
        lead, rest = halves(decay[t])
        for h in range(HEADS):
            cols = slice(h * DK, (h + 1) * DK)
            f[h, ROW_HI + 2 * t : ROW_HI + 2 * t + 2, :] = lead.astype(F32)[:, cols]
            f[h, ROW_LO + 2 * t : ROW_LO + 2 * t + 2, :] = rest.astype(F32)[:, cols]
    for h in range(HEADS):
        s2[h] = f[h].astype(BF16)


def middle(h, jg, r1, r2, weight, rate, targets, b1, b2, f1, f2, mem, xt):
    def widen(i, _):
        f2[pl.ds(pl.multiple_of(i * ROWS, 8), ROWS), :] = r2[i].astype(F32)
        f1[pl.ds(pl.multiple_of(i * 16, 8), 16), :] = r1[i].astype(F32)
        return 0

    lax.fori_loop(0, GROUPS, widen, 0)

    def both(row, step):
        return jnp.concatenate(
            [f2[pl.ds(row + s * step, GROUPS, stride=ROWS), :] for s in range(2)], axis=0
        )

    for j in range(JW):
        rows = [f1[pl.ds(s * JW + j, GROUPS, stride=16), :] for s in range(2)]
        mem[j] = jnp.concatenate(rows, axis=0).T

    taps = weight[...].T
    eye = jnp.where(iota((SLOTS, SLOTS), 0) == iota((SLOTS, SLOTS), 1), 1.0, 0.0).astype(BF16)
    mine = pl.ds(pl.multiple_of(jg * JW, JW), JW)

    def parts_of(w, at):
        x = jnp.concatenate([both(ROW_X + w * 6 + part, 3) for part in range(3)], axis=1)
        return contract(x.astype(BF16), at, 0, 0)

    for w in range(HIST):
        xt[w] = parts_of(w, eye)
    tap_rows = [[taps[:, 3 * n + part : 3 * n + part + 1] for part in range(3)] for n in range(TAPS)]
    xt[HIST, 0:DK, 0 : TAPS * 3] = taps[:, 0 : TAPS * 3]
    value_taps = [
        xt[HIST, mine, 3 * n + 2 : 3 * n + 3] for n in range(TAPS)
    ]

    def split(ref_index):
        return [
            xt[ref_index, 0:DK, :],
            xt[ref_index, DK : 2 * DK, :],
            xt[ref_index, pl.ds(pl.multiple_of(2 * DK + jg * JW, JW), JW), :],
        ]

    hist = [split(w) for w in range(HIST)]
    misc = jnp.concatenate(
        [f2[pl.ds(ROW_MISC + s, GROUPS, stride=ROWS), :] for s in range(2)], axis=0
    ).astype(BF16)
    place = eye
    readouts = []
    for t in range(STEPS):
        move = jnp.where(iota((SLOTS, SLOTS), 0) == targets[t : t + 1, :], 1.0, 0.0).astype(BF16)
        place = move if t == 0 else contract(move, place, 1, 0).astype(BF16)
        xt[HIST] = parts_of(t + HIST, place)
        new = split(HIST)
        lead, rest = both(ROW_HI + 2 * t, 1).astype(BF16), both(ROW_LO + 2 * t, 1).astype(BF16)
        decay = contract(lead, place, 0, 0) + contract(rest, place, 0, 0)
        flags = contract(misc, place, 0, 0)[t * 8 : t * 8 + 8, :]
        alive = flags[0:1] > 0.5
        strength = jnp.where(alive, sigmoid(flags[1:2] + flags[2:3]), 0.0)
        retain = jnp.where(alive, jnp.exp(-rate * softplus(decay)), 1.0)
        window = hist + [new]
        acts = []
        for part in range(3):
            weights = [value_taps[n] if part == 2 else tap_rows[n][part] for n in range(TAPS)]
            total = window[0][part] * weights[0]
            for n in range(1, TAPS):
                total = total + window[n][part] * weights[n]
            acts.append(total / (1.0 + jnp.exp(-total)))
        hist = [
            [jnp.where(alive, window[n + 1][part], window[n][part]) for part in range(3)]
            for n in range(HIST)
        ]
        query, key, value = acts
        query = query / jnp.sqrt(jnp.sum(query * query, axis=0, keepdims=True) + EPS)
        key = key / jnp.sqrt(jnp.sum(key * key, axis=0, keepdims=True) + EPS)
        rows = []
        for j in range(JW):
            decayed = retain * mem[j]
            recalled = jnp.sum(key * decayed, axis=0, keepdims=True)
            updated = decayed + key * (strength * (value[j : j + 1] - recalled))
            mem[j] = updated
            rows.append(jnp.sum(query * updated, axis=0, keepdims=True) * DK**-0.5)
        lead, rest = halves(jnp.concatenate(rows, axis=0))
        readouts.append(contract(place, lead, 1, 1) + contract(place, rest, 1, 1))

    for j in range(JW):
        final = contract(place, mem[j].astype(BF16), 1, 1)
        for s in range(2):
            f1[pl.ds(s * JW + j, GROUPS, stride=16), :] = final[s * GROUPS : (s + 1) * GROUPS]
    xt[HIST, 0:DK, :] = jnp.zeros((DK, SLOTS), F32)
    for n in range(HIST):
        for part in range(3):
            block = hist[n][part]
            if part < 2:
                xt[HIST, DK * (part + 1) : DK * (part + 2), :] = block
                block = xt[HIST, pl.ds(pl.multiple_of(DK * (part + 1) + jg * JW, JW), JW), :]
            at = (n * 3 + part) * JW
            xt[HIST, at : at + JW, :] = block
    kept = contract(place, xt[HIST, 0:DK, :].astype(BF16), 1, 1)
    tail = jnp.concatenate(readouts + [jnp.zeros((SLOTS, DK - BLOCKS * JW), F32)], axis=1)
    xt[HIST, 0:SLOTS, :] = kept
    xt[HIST, 0:SLOTS, CONV * JW : DK] = tail
    for s in range(2):
        b2[pl.ds(s, GROUPS, stride=2), :] = xt[HIST, s * GROUPS : (s + 1) * GROUPS, :]

    def narrow(i, _):
        b1[i] = f1[pl.ds(pl.multiple_of(i * 16, 8), 16), :].astype(BF16)
        return 0

    lax.fori_loop(0, GROUPS, narrow, 0)


def finish(a1, a2, gate, gain, live, weight, states, conv, partial, fc, fg):
    for h in range(HEADS):
        pieces = [a1[holder(h, jg)].astype(F32) for jg in range(JG)]
        for s in range(2):
            states[s, h] = jnp.concatenate([p[s * JW : (s + 1) * JW] for p in pieces], axis=0).T
    both = jnp.concatenate([a2[pl.ds(s, GROUPS, stride=2), :] for s in range(2)], axis=0)
    lead, rest = halves(both)
    wide = (DK, BLOCKS * DK)
    source = (iota(wide, 1) // DK) * JW + iota(wide, 1) % JW
    spread = jnp.where(iota(wide, 0) == source, 1.0, 0.0).astype(BF16)
    every = contract(lead, spread, 1, 0) + contract(rest, spread, 1, 0)
    own = iota((SLOTS, DK), 0) % GROUPS
    own = (own // 32) * 8 + own % 8
    own = jnp.where(own == iota((SLOTS, DK), 1) // JW, 1.0, 0.0)

    def block(b):
        picked = every[:, b * DK : (b + 1) * DK] * own
        rows = []
        for s in range(2):
            for h in range(HEADS):
                at = s * GROUPS + h * 8
                rows.append(
                    jnp.sum(picked[at : at + 8] + picked[at + 32 : at + 40], axis=0, keepdims=True)
                )
        return jnp.concatenate(rows, axis=0)

    for n in range(HIST):
        for part in range(3):
            kept = block(n * 3 + part)
            for s in range(2):
                for h in range(HEADS):
                    r = s * HEADS + h
                    fc[s, n, part : part + 1, h * DK : (h + 1) * DK] = kept[r : r + 1]
    conv[...] = fc[...].astype(BF16)

    fg[...] = jnp.zeros_like(fg)
    for t in range(STEPS):
        readout = block(CONV + t)
        scaling = lax.rsqrt(jnp.sum(readout * readout, axis=1, keepdims=True) / DK + EPS)
        logits = gate[t].astype(F32)
        gates = sigmoid(
            jnp.concatenate(
                [logits[s : s + 1, h * DK : (h + 1) * DK] for s in range(2) for h in range(HEADS)],
                axis=0,
            )
        )
        gated = readout * scaling * gain[...] * gates
        for s in range(2):
            alive = jnp.where(live[t, 0] > s, 1.0, 0.0)
            for h in range(HEADS):
                r = s * HEADS + h
                fg[2 * t + s : 2 * t + s + 1, h * DK : (h + 1) * DK] = gated[r : r + 1] * alive
    total = jnp.dot(fg[...].astype(BF16), weight[...], preferred_element_type=F32)
    width = partial.shape[2]
    share = total.shape[1] // partial.shape[0]
    for d in range(partial.shape[0]):
        turned = total if d == 0 else pltpu.roll(total, total.shape[1] - d * share, 1)
        partial[d] = turned[:, :width].astype(BF16)


def greet(axis, count):
    me = lax.axis_index(axis)
    barrier = pltpu.get_barrier_semaphore()

    def signal(k, _):
        pl.semaphore_signal(
            barrier,
            inc=1,
            device_id={axis: lax.rem(me + k, count)},
            device_id_type=pl.DeviceIdType.MESH,
        )
        return 0

    lax.fori_loop(1, count, signal, 0)
    pl.semaphore_wait(barrier, count - 1)
    return me


def remote(axis, peer, src, dst, send, recv):
    return pltpu.make_async_remote_copy(
        src_ref=src,
        dst_ref=dst,
        send_sem=send,
        recv_sem=recv,
        device_id={axis: peer},
        device_id_type=pl.DeviceIdType.MESH,
    )


def spread_kernel(s1, s2, r1, r2, sems, own):
    me = greet("rep", GROUPS)
    head = piece_of(me)[0]
    keep = [
        pltpu.make_async_copy(s1.at[me], r1.at[me], own.at[0]),
        pltpu.make_async_copy(s2.at[head], r2.at[me], own.at[1]),
    ]
    for copy in keep:
        copy.start()

    def send(k, _):
        p = lax.rem(me + k, GROUPS)
        remote("rep", p, s2.at[piece_of(p)[0]], r2.at[me], sems.at[2], sems.at[3]).start()
        remote("rep", p, s1.at[p], r1.at[me], sems.at[0], sems.at[1]).start()
        return 0

    lax.fori_loop(1, GROUPS, send, 0)
    for copy in keep:
        copy.wait()
    most = pl.ds(0, GROUPS - 1)
    for buf, n in ((r1, 0), (r2, 2)):
        done = remote("rep", me, buf.at[most], buf.at[most], sems.at[n], sems.at[n + 1])
        done.wait_send()
        done.wait_recv()


def swap_kernel(axis, count, *refs):
    pairs = (len(refs) - 2) // 2
    sources, lands, sems, own = refs[:pairs], refs[pairs : 2 * pairs], refs[-2], refs[-1]
    me = greet(axis, count)
    keep = [
        pltpu.make_async_copy(s.at[me], d.at[me], own.at[n])
        for n, (s, d) in enumerate(zip(sources, lands))
    ]
    for copy in keep:
        copy.start()

    def send(k, _):
        p = lax.rem(me + k, count)
        for n, (s, d) in enumerate(zip(sources, lands)):
            remote(axis, p, s.at[p], d.at[me], sems.at[2 * n], sems.at[2 * n + 1]).start()
        return 0

    lax.fori_loop(1, count, send, 0)
    for copy in keep:
        copy.wait()
    most = pl.ds(0, count - 1)
    for n, d in enumerate(lands):
        done = remote(axis, me, d.at[most], d.at[most], sems.at[2 * n], sems.at[2 * n + 1])
        done.wait_send()
        done.wait_recv()


VMEM = pl.BlockSpec(memory_space=pltpu.VMEM)
SMEM = pl.BlockSpec(memory_space=pltpu.SMEM)
ANY = pl.BlockSpec(memory_space=pl.ANY)
BIG = 48 * 1024 * 1024


def shape(dims, kind):
    return jax.ShapeDtypeStruct(dims, kind)


def do_pack(states, conv, proj, decay, beta, live):
    return pl.pallas_call(
        pack,
        out_shape=(shape((GROUPS, 16, DK), BF16), shape((HEADS, ROWS, DK), BF16)),
        in_specs=[VMEM] * 4 + [SMEM] * 2,
        out_specs=(VMEM, VMEM),
        scratch_shapes=[pltpu.VMEM((HEADS, ROWS, DK), F32)],
        compiler_params=pltpu.CompilerParams(vmem_limit_bytes=BIG),
        name="pack",
    )(states, conv, proj, decay, beta, live)


def do_spread(s1, s2):
    return pl.pallas_call(
        spread_kernel,
        out_shape=(shape((GROUPS, 16, DK), BF16), shape((GROUPS, ROWS, DK), BF16)),
        in_specs=[ANY] * 2,
        out_specs=(ANY, ANY),
        scratch_shapes=[pltpu.SemaphoreType.DMA((4,)), pltpu.SemaphoreType.DMA((2,))],
        compiler_params=pltpu.CompilerParams(collective_id=0, has_side_effects=True),
        name="spread",
    )(s1, s2)


def middle_kernel(where, r1, r2, weight, rate, targets, *rest):
    middle(where[0], where[1], r1, r2, weight, rate[where[0]], targets, *rest)


def do_middle(where, r1, r2, weight, rate, targets):
    return pl.pallas_call(
        middle_kernel,
        out_shape=(shape((GROUPS, 16, DK), BF16), shape((GROUPS * 2, DK), F32)),
        in_specs=[SMEM, VMEM, VMEM, VMEM, SMEM, VMEM],
        out_specs=(VMEM, VMEM),
        scratch_shapes=[
            pltpu.VMEM((GROUPS * 16, DK), F32),
            pltpu.VMEM((GROUPS * ROWS, DK), F32),
            pltpu.VMEM((JW, DK, SLOTS), F32),
            pltpu.VMEM((HIST + 1, 3 * DK, SLOTS), F32),
        ],
        compiler_params=pltpu.CompilerParams(vmem_limit_bytes=BIG),
        name="middle",
    )(where, r1, r2, weight, rate, targets)


def do_finish(a1, a2, gate, gain, live, weight, heads_axis):
    width = -(-(weight.shape[1] // heads_axis) // DK) * DK
    return pl.pallas_call(
        finish,
        out_shape=(
            shape((2, HEADS, DK, DK), F32),
            shape((2, HIST, 3, HEADS * DK), BF16),
            shape((heads_axis, 16, width), BF16),
        ),
        in_specs=[VMEM] * 4 + [SMEM] + [VMEM],
        out_specs=(VMEM, VMEM, VMEM),
        scratch_shapes=[
            pltpu.VMEM((2, HIST, 3, HEADS * DK), F32),
            pltpu.VMEM((16, HEADS * DK), F32),
        ],
        compiler_params=pltpu.CompilerParams(vmem_limit_bytes=BIG),
        name="finish",
    )(a1, a2, gate, gain, live, weight)


def do_swap(axis, count, tag, *sources):
    return pl.pallas_call(
        functools.partial(swap_kernel, axis, count),
        out_shape=tuple(shape(s.shape, s.dtype) for s in sources),
        in_specs=[ANY] * len(sources),
        out_specs=tuple([ANY] * len(sources)),
        scratch_shapes=[
            pltpu.SemaphoreType.DMA((2 * len(sources),)),
            pltpu.SemaphoreType.DMA((len(sources),)),
        ],
        compiler_params=pltpu.CompilerParams(collective_id=tag, has_side_effects=True),
        name="swap%d" % tag,
    )(*sources)


def local(
    heads_axis,
    states,
    conv_states,
    projected,
    conv_weight,
    decay_input,
    decay_rate,
    beta_logit,
    out_gate,
    norm_gain,
    out_weight,
    destinations,
    live_counts,
):
    me = lax.axis_index("rep")
    head, jg = piece_of(me)
    s1, s2 = do_pack(states, conv_states, projected, decay_input, beta_logit, live_counts)
    r1, r2 = do_spread(s1, s2)
    targets = destinations.reshape(STEPS, GROUPS, 2).transpose(0, 2, 1).reshape(STEPS, SLOTS)
    targets = (targets % 2) * GROUPS + targets // 2
    weight = lax.dynamic_slice_in_dim(conv_weight, head * DK, DK, axis=2).reshape(TAPS * 3, DK)
    weight = jnp.pad(weight, ((0, 16 - TAPS * 3), (0, 0)))
    where = jnp.stack([head, jg]).astype(jnp.int32)
    b1, b2 = do_middle(where, r1, r2, weight, decay_rate, targets)
    a1, a2 = do_swap("rep", GROUPS, 1, b1, b2.reshape(GROUPS, 2, DK))
    states_out, conv_out, partial = do_finish(
        a1,
        a2.reshape(GROUPS * 2, DK),
        out_gate,
        norm_gain.reshape(1, DK),
        live_counts,
        out_weight,
        heads_axis,
    )
    (shares,) = do_swap("head", heads_axis, 2, partial)
    share = out_weight.shape[1] // heads_axis
    out = jnp.sum(shares.astype(F32), axis=0)[: 2 * STEPS, :share].astype(BF16)
    return out.reshape(STEPS, 2, share), states_out, conv_out


def solution(mesh):
    placed = (
        P("rep", "head", None, None),
        P("rep", None, None, "head"),
        P(None, "rep", None, "head"),
        P(None, None, "head"),
        P(None, "rep", "head"),
        P("head"),
        P(None, "rep", "head"),
        P(None, "rep", "head"),
        P(),
        P("head", None),
        P(),
        P(None, "rep"),
    )
    return jax.shard_map(
        functools.partial(local, mesh.shape["head"]),
        mesh=mesh,
        in_specs=placed,
        out_specs=(
            P(None, "rep", "head"),
            P("rep", "head", None, None),
            P("rep", None, None, "head"),
        ),
        check_vma=False,
    )
```

time: 919 us -> 107 us (0.12); the launches traced: 902 us -> 106 us
  waiting for transfers between devices: 408 us -> 0 us
  starting transfers between devices: 200 us -> 0 us
  local copies, waits for them, and re-layouts: 173 us -> 16.5 us
  other arithmetic: 91.2 us -> 1.01 us
  Pallas kernels: 0 us -> 87.8 us
  between operations: 16.1 us -> 0.84 us
  matrix products: 13.3 us -> 0 us
    unnamed x12 -> x0, waiting for transfers between devices: 207 us -> none
    all_to_all x24 -> x0, waiting for transfers between devices: 201 us -> none  [the longest x6 101 us: move_every(): lax.all_to_all(history.astype(jnp.float32), 'rep', split_axis=2, concat_a...]
    all_to_all x24 -> x0, starting transfers between devices: 200 us -> none  [the longest x6 56.9 us: move_every(): lax.all_to_all(spread_memory[source], 'rep', split_axis=0, concat_axis=2,...]
    pallas_call x0 -> x6, Pallas kernels: none -> 87.8 us  [the longest x1 48.6 us: do_spread(): pl.pallas_call(spread_kernel, out_shape=(shape((GROUPS, 16, DK), BF16), s...]
    reduce_sum x30 -> x1, other arithmetic: 41.3 us -> 0.91 us  [local(): out = jnp.sum(shares.astype(F32), axis=0)[:2 * STEPS, :share].astype(BF16)]
    all_to_all x47 -> x0, local copies, waits for them, and re-layouts: 31.4 us -> none  [the longest x17 11.7 us: move_every(): lax.all_to_all(memory, 'rep', split_axis=2, concat_axis=0, tiled=True)]
    div x12 -> x0, local copies, waits for them, and re-layouts: 28.6 us -> none  [unit_rows(): vectors / jnp.sqrt(jnp.sum(vectors * vectors, axis=-1, keepdims=True) + E...]
    gather x12 -> x0, local copies, waits for them, and re-layouts: 21.5 us -> none  [the longest x6 12.7 us: move_every(): spread_memory[source]]
  transfers between devices with their start and end apart: 30 -> 0, of which waited for: 22 -> 0; matrix products, arithmetic and copies ran while one was open for 22% -> 0% of each run, Pallas kernels for 0% -> 0%
where the time goes in v1:
time: 107 us; the launch traced here: 106 us
  Pallas kernels  87.8 us (82%)
  local copies, waits for them, and re-layouts  16.5 us (15%)
    pallas_call x1, Pallas kernels, do_spread(): pl.pallas_call(spread_kernel, out_shape=(shape((GROUPS, 16, DK), BF16), s...  48.6 us
    pallas_call x2, Pallas kernels, do_swap(): pl.pallas_call(functools.partial(swap_kernel, axis, count), out_shape=tup...  31.1 us
    unnamed x38, local copies, waits for them, and re-layouts  15.7 us
    pallas_call x1, Pallas kernels, do_middle(): pl.pallas_call(middle_kernel, out_shape=(shape((GROUPS, 16, DK), BF16), s...  5.16 us
    pallas_call x1, Pallas kernels, do_finish(): pl.pallas_call(finish, out_shape=(shape((2, HEADS, DK, DK), F32), shape((...  2.16 us

profile of v1, /device:TPU:1, one launch (start us, length us, event | category | flops | bytes accessed | tf_op | source)
XLA Modules:
  0.0 106.2 jit_solution(9460094458330458816)
XLA Ops:
  0.6 0.0 copy-start
  0.7 0.1 pad_add_fusion.where
  0.8 0.9 copy.23.conv
  1.7 0.8 copy.24.proj
  2.4 0.8 copy.25.beta
  3.2 0.7 copy.26.live
  4.0 1.0 copy-done.3
  5.0 0.7 copy-done.12
  5.8 0.9 pack.1
  6.6 0.7 copy-done.6
  7.3 0.6 copy-done.9
  7.9 48.6 %spread.1 = (bf16[64,16,128]{2,1,0:T(8,128)(2,1)}, bf16[64,80,128]{2,1,0:T(8,128)(2,1)}) custom-call(bf16[64,16,128]{2,1,0:T(8,128)(2,1)} %copy-done.6, bf16[4,80,128]{2,1,0:T(8,128)(2,1)} %copy-done.9), custom_call_target="tpu_custom_call" | custom-call | tf_op jit(solution)/shard_map/spread/pallas_call | solution.py:365
  56.6 0.8 copy.28
  57.4 0.1 copy.29
  57.5 0.1 reshape.29
  57.6 1.3 %copy-done.2 = bf16[64,80,128]{2,1,0:T(8,128)(2,1)S(1)} copy-done((bf16[64,80,128]{2,1,0:T(8,128)(2,1)S(1)}, bf16[64,80,128]{2,1,0:T(8,128)(2,1)}, u32[]{:S(2)}) %copy-start.2) | copy-done | bytes 1310744
  58.9 0.9 copy-done.7
  59.9 0.7 copy-done.14
  60.5 5.2 %middle.1 = (bf16[64,16,128]{2,1,0:T(8,128)(2,1)S(1)}, f32[128,128]{1,0:T(8,128)S(1)}) custom-call(s32[2]{0:T(128)S(1)} %pad_add_fusion.where, bf16[64,16,128]{2,1,0:T(8,128)(2,1)S(1)} %copy-done.7, bf16[64,80,128]{2,1,0:T(8,128)(2,1)S(1)} %copy-done.2, f32[16,128]{1,0:T(8,128)S(1)} %pad.4.weight, f32[4]{0:T(128)S(1)} %copy-done.14, s32[6,128]{1,0:T(8,128)S(1)} %fusion.1.targets), custom_call_target="tpu_custom_call" | custom-call | tf_op jit(solution)/shard_map/middle/pallas_call | solution.py:381
  65.7 0.7 copy-done.5
  66.4 0.6 copy-done.10
  67.0 21.6 %swap1.1 = (bf16[64,16,128]{2,1,0:T(8,128)(2,1)}, f32[64,2,128]{2,1,0:T(2,128)}) custom-call(bf16[64,16,128]{2,1,0:T(8,128)(2,1)} %copy-done.5, f32[64,2,128]{2,1,0:T(2,128)} %bitcast.9), custom_call_target="tpu_custom_call" | custom-call | tf_op jit(solution)/shard_map/swap1/pallas_call | solution.py:418
  88.6 0.9 copy-done.4
  89.6 0.8 copy-done.11
  90.4 0.7 copy-done.13
  91.1 0.7 copy-done.15
  91.8 2.2 %finish.1 = (f32[2,4,128,128]{3,2,1,0:T(8,128)}, bf16[2,3,3,512]{3,2,1,0:T(4,128)(2,1)S(1)}, bf16[8,16,384]{2,1,0:T(8,128)(2,1)S(1)}) custom-call(bf16[64,16,128]{2,1,0:T(8,128)(2,1)S(1)} %copy-done.4, f32[128,128]{1,0:T(8,128)S(1)} %bitcast.10, bf16[6,2,512]{2,1,0:T(2,128)(2,1)S(1)} %copy-done.13, f32[1,128]{1,0:T(1,128)S(1)} %bitcast.11, ...), custom_call_target="tpu_custom_call" | custom-call | tf_op jit(solution)/shard_map/finish/pallas_call | solution.py:399
  93.9 0.6 copy-done.8
  94.6 9.5 %swap2.1 = bf16[8,16,384]{2,1,0:T(8,128)(2,1)} custom-call(bf16[8,16,384]{2,1,0:T(8,128)(2,1)} %copy-done.8), custom_call_target="tpu_custom_call" | custom-call | tf_op jit(solution)/shard_map/swap2/pallas_call | solution.py:418
  104.1 0.9 reduce
  105.0 0.6 reshape.33
  105.6 0.6 copy.31
  (22 shorter events, 0.1 us)
Async XLA Ops:
  0.6 55.9 %copy-start = (f32[4,3,512]{2,0,1:T(4,128)S(1)}, f32[4,3,512]{2,0,1:T(4,128)}, u32[]{:S(2)}) copy-start(f32[4,3,512]{2,0,1:T(4,128)} %param.15) | copy-start | bytes 73732
  0.6 88.0 %copy-start.1 = (bf16[512,2304]{1,0:T(8,128)(2,1)S(1)}, bf16[512,2304]{1,0:T(8,128)(2,1)}, u32[]{:S(2)}) copy-start(bf16[512,2304]{1,0:T(8,128)(2,1)} %weight.1) | copy-start | bytes 7077892
  4.0 1.0 copy-start.3
  5.0 0.7 copy-start.12
  6.6 0.7 copy-start.6
  7.3 0.6 copy-start.9
  57.6 1.3 %copy-start.2 = (bf16[64,80,128]{2,1,0:T(8,128)(2,1)S(1)}, bf16[64,80,128]{2,1,0:T(8,128)(2,1)}, u32[]{:S(2)}) copy-start(bf16[64,80,128]{2,1,0:T(8,128)(2,1)} %get-tuple-element.17.r2) | copy-start | bytes 3932164
  58.9 0.9 copy-start.7
  59.8 0.7 copy-start.14
  65.7 0.7 copy-start.5
  66.4 0.6 copy-start.10
  88.6 1.0 copy-start.4
  89.6 0.8 copy-start.11
  90.4 0.7 copy-start.13
  91.1 0.7 copy-start.15
  93.9 0.6 copy-start.8

commit v2 on v0

v2 whole, which is shorter than its diff:
```python
import functools

import jax
import jax.numpy as jnp
from jax import lax
from jax.experimental import pallas as pl
from jax.experimental.pallas import tpu as pltpu
from jax.sharding import PartitionSpec as P

F32, BF16 = jnp.float32, jnp.bfloat16
STEPS, TAPS = 6, 4
HIST = TAPS - 1
ZS, XS, CS = 8, 4, 2
GROUPS, HEADS, DK = 64, 4, 128
SLOTS = 2 * GROUPS
JG, JW = 16, 8
WIN = HIST + STEPS
ROW_HI = WIN * 4
ROW_LO = ROW_HI + 2 * STEPS
ROWS = 64
LANE_ALIVE = WIN * JW
LANE_BETA = LANE_ALIVE + 8
CONV = 3 * HIST
BLOCKS = CONV + STEPS
EPS = 1e-6


def holder(h, jg):
    return (jg % 8) * ZS + (jg // 8) * HEADS + h


def iota(shape, dim):
    return lax.broadcasted_iota(jnp.int32, shape, dim)


def contract(a, b, da, db):
    return lax.dot_general(a, b, (((da,), (db,)), ((), ())), preferred_element_type=F32)


def halves(x):
    lead = x.astype(BF16)
    return lead, (x - lead.astype(F32)).astype(BF16)


def sigmoid(x):
    return 1.0 / (1.0 + jnp.exp(-x))


def softplus(x):
    return jnp.maximum(x, 0.0) + jnp.log1p(jnp.exp(-jnp.abs(x)))


def inner(slot):
    group = slot >> 1
    return ((slot & 1) << 6) + ((group & 1) << 5) + (((group >> 1) & 3) << 3) + (group >> 3)


def own_lanes():
    group = iota((SLOTS, DK), 0) & 63
    piece = (group >> 3) + ((group & 4) << 1)
    return jnp.where(piece == iota((SLOTS, DK), 1) >> 3, 1.0, 0.0)


def by_head(x):
    return [
        jnp.concatenate([x[s : s + 1, h * DK : (h + 1) * DK] for h in range(HEADS)], axis=0)
        for s in range(2)
    ]


def pack_inputs(conv, proj, decay, s2, f):
    for w in range(WIN):
        for part in range(2):
            block = (conv[w, part] if w < HIST else proj[w - HIST, part]).astype(F32)
            at = (w * 2 + part) * 2
            for h in range(HEADS):
                f[h, at : at + 2, :] = block[:, h * DK : (h + 1) * DK]
    for t in range(STEPS):
        lead, rest = halves(decay[t])
        lead, rest = lead.astype(F32), rest.astype(F32)
        for h in range(HEADS):
            cols = slice(h * DK, (h + 1) * DK)
            f[h, ROW_HI + 2 * t : ROW_HI + 2 * t + 2, :] = lead[:, cols]
            f[h, ROW_LO + 2 * t : ROW_LO + 2 * t + 2, :] = rest[:, cols]
    for h in range(HEADS):
        f[h, ROW_LO + 2 * STEPS : ROWS, :] = jnp.zeros((ROWS - ROW_LO - 2 * STEPS, DK), F32)
        s2[h] = f[h].astype(BF16)


def pack_values(conv, proj, beta, live, s3):
    mask = own_lanes()
    parts = []
    for w in range(WIN):
        block = (conv[w, 2] if w < HIST else proj[w - HIST, 2]).astype(F32)
        rows = []
        for four in by_head(block):
            rows += [four] * (2 * ZS)
        parts.append((jnp.concatenate(rows, axis=0) * mask).astype(BF16))
    shape = (WIN * DK, DK)
    place = jnp.where(((iota(shape, 0) >> 7) << 3) + (iota(shape, 0) & 7) == iota(shape, 1), 1.0, 0.0)
    packed = contract(jnp.concatenate(parts, axis=1), place.astype(BF16), 1, 0)
    for s in range(2):
        alive = jnp.where(live[...] > s, 1.0, 0.0)
        row = jnp.concatenate(
            [
                jnp.zeros((HEADS, LANE_ALIVE), F32),
                jnp.broadcast_to(alive, (HEADS, STEPS)),
                jnp.zeros((HEADS, 8 - STEPS), F32),
                beta[s],
                jnp.zeros((HEADS, DK - LANE_BETA - STEPS), F32),
            ],
            axis=1,
        )
        rest = jnp.concatenate([row] * (2 * ZS), axis=0)
        s3[:, s, :] = packed[s * GROUPS : (s + 1) * GROUPS] + rest


def pack_states(states, s1):
    for h in range(HEADS):
        first, second = states[0, h].T, states[1, h].T
        for jg in range(JG):
            rows = slice(jg * JW, (jg + 1) * JW)
            s1[holder(h, jg)] = jnp.concatenate([first[rows], second[rows]], axis=0).astype(BF16)


def widen_inputs(r2, f2, core, x):
    def one(i, _):
        at = pl.multiple_of(((core * XS + x) * ZS + i) * ROWS, ROWS)
        f2[pl.ds(at, ROWS), :] = r2[core, x, i].astype(F32)
        return 0

    lax.fori_loop(0, ZS, one, 0)


def enter_states(r1, f1, mem):
    def one(i, _):
        f1[pl.ds(pl.multiple_of(i * 16, 16), 16), :] = r1[i].astype(F32)
        return 0

    lax.fori_loop(0, GROUPS, one, 0)
    for j in range(JW):
        rows = [f1[pl.ds(s * JW + j, GROUPS, stride=16), :] for s in range(2)]
        mem[j] = jnp.concatenate(rows, axis=0).T


def find_places(targets, places):
    square = (SLOTS, SLOTS)
    back = jnp.where(inner(iota(square, 0)) == iota(square, 1), 1.0, 0.0).astype(BF16)
    held = back
    for t in range(STEPS):
        move = jnp.where(iota(square, 0) == inner(targets[t : t + 1, :]), 1.0, 0.0).astype(BF16)
        place = contract(move, held, 1, 0).astype(BF16)
        places[t] = place
        if t < STEPS - 1:
            held = contract(back, place, 1, 0).astype(BF16)


def run_steps(jg, f2, r3, weight, rate, places, mem, xt):
    def both(row):
        return jnp.concatenate(
            [f2[pl.ds(row + s, GROUPS, stride=ROWS), :] for s in range(2)], axis=0
        )

    square = (SLOTS, SLOTS)
    eye = jnp.where(iota(square, 0) == iota(square, 1), 1.0, 0.0).astype(BF16)
    taps = [weight[part].T for part in range(3)]
    xt[0:DK, 0:TAPS] = taps[2]
    mine = pl.ds(pl.multiple_of(jg * JW, JW), JW)
    value_taps = xt[mine, 0:TAPS]
    values = jnp.concatenate([r3[:, s, :] for s in range(2)], axis=0)
    lead3, rest3 = halves(values)

    def pair(w, extra, at):
        x = jnp.concatenate([both(w * 4), both(w * 4 + 2)] + extra, axis=1)
        return contract(x.astype(BF16), at, 0, 0)

    start = contract(lead3, eye, 0, 0)
    hist = []
    for w in range(HIST):
        two = pair(w, [], eye)
        hist.append([two[:DK], two[DK:], start[w * JW : (w + 1) * JW]])
    readouts = []
    for t in range(STEPS):
        place = places[t]
        four = pair(t + HIST, [both(ROW_HI + 2 * t), both(ROW_LO + 2 * t)], place)
        decay = four[2 * DK : 3 * DK] + four[3 * DK :]
        small = contract(lead3, place, 0, 0) + contract(rest3, place, 0, 0)
        new = [four[:DK], four[DK : 2 * DK], small[(t + HIST) * JW : (t + HIST + 1) * JW]]
        alive = small[LANE_ALIVE + t : LANE_ALIVE + t + 1] > 0.5
        logit = small[LANE_BETA + t : LANE_BETA + t + 1]
        strength = jnp.where(alive, sigmoid(logit), 0.0)
        retain = jnp.where(alive, jnp.exp(-rate * softplus(decay)), 1.0)
        window = hist + [new]
        acts = []
        for part in range(3):
            cols = value_taps if part == 2 else taps[part]
            total = window[0][part] * cols[:, 0:1]
            for n in range(1, TAPS):
                total = total + window[n][part] * cols[:, n : n + 1]
            acts.append(total / (1.0 + jnp.exp(-total)))
        hist = [
            [jnp.where(alive, window[n + 1][part], window[n][part]) for part in range(3)]
            for n in range(HIST)
        ]
        query, key, value = acts
        query = query / jnp.sqrt(jnp.sum(query * query, axis=0, keepdims=True) + EPS)
        key = key / jnp.sqrt(jnp.sum(key * key, axis=0, keepdims=True) + EPS)
        rows = []
        for j in range(JW):
            decayed = retain * mem[j]
            recalled = jnp.sum(key * decayed, axis=0, keepdims=True)
            updated = decayed + key * (strength * (value[j : j + 1] - recalled))
            mem[j] = updated
            rows.append(jnp.sum(query * updated, axis=0, keepdims=True) * DK**-0.5)
        lead, rest = halves(jnp.concatenate(rows, axis=0))
        readouts.append(contract(place, lead, 1, 1) + contract(place, rest, 1, 1))
    kept = []
    for n in range(HIST):
        for part in range(3):
            block = hist[n][part]
            if part < 2:
                xt[...] = block
                block = xt[mine, :]
            kept.append(block)
    kept = jnp.concatenate(kept, axis=0).astype(BF16)
    kept = contract(places[STEPS - 1], kept, 1, 1)
    pad = jnp.zeros((SLOTS, DK - BLOCKS * JW), F32)
    return jnp.concatenate([kept] + readouts + [pad], axis=1)


def leave_states(place, mem, f1, b1):
    for j in range(JW):
        final = contract(place, mem[j].astype(BF16), 1, 1)
        for s in range(2):
            f1[pl.ds(s * JW + j, GROUPS, stride=16), :] = final[s * GROUPS : (s + 1) * GROUPS]

    def one(i, _):
        b1[i] = f1[pl.ds(pl.multiple_of(i * 16, 16), 16), :].astype(BF16)
        return 0

    lax.fori_loop(0, GROUPS, one, 0)


def finish_rows(a2, gate, gain, live, weight, conv, partial, fc, fg):
    lead, rest = halves(jnp.concatenate([a2[:, s, :] for s in range(2)], axis=0))
    wide = (DK, BLOCKS * DK)
    source = ((iota(wide, 1) >> 7) << 3) + (iota(wide, 1) & 7)
    spread = jnp.where(iota(wide, 0) == source, 1.0, 0.0).astype(BF16)
    every = contract(lead, spread, 1, 0) + contract(rest, spread, 1, 0)
    mask = own_lanes()

    def block(b):
        picked = every[:, b * DK : (b + 1) * DK] * mask
        rows = []
        for s in range(2):
            total = picked[s * GROUPS : s * GROUPS + ZS]
            for n in range(1, GROUPS // ZS):
                total = total + picked[s * GROUPS + n * ZS : s * GROUPS + (n + 1) * ZS]
            rows.append(total[:HEADS] + total[HEADS:])
        return jnp.concatenate(rows, axis=0)

    fg[...] = jnp.zeros_like(fg)
    second = iota((2 * HEADS, DK), 0) >> 2
    for t in range(STEPS):
        readout = block(CONV + t)
        scaling = lax.rsqrt(jnp.sum(readout * readout, axis=1, keepdims=True) / DK + EPS)
        gates = sigmoid(jnp.concatenate(by_head(gate[t].astype(F32)), axis=0))
        gated = readout * scaling * gain[...] * gates
        gated = jnp.where(live[0:1, t : t + 1] > second, gated, 0.0)
        for s in range(2):
            for h in range(HEADS):
                r = s * HEADS + h
                fg[2 * t + s : 2 * t + s + 1, h * DK : (h + 1) * DK] = gated[r : r + 1]
    total = jnp.dot(fg[...].astype(BF16), weight[...], preferred_element_type=F32)
    width = partial.shape[2]
    share = total.shape[1] // partial.shape[0]
    for d in range(partial.shape[0]):
        turned = total if d == 0 else pltpu.roll(total, total.shape[1] - d * share, 1)
        partial[d] = turned[:, :width].astype(BF16)
    for n in range(HIST):
        for part in range(3):
            kept = block(n * 3 + part)
            for s in range(2):
                for h in range(HEADS):
                    r = s * HEADS + h
                    fc[n, part, s : s + 1, h * DK : (h + 1) * DK] = kept[r : r + 1]
    conv[...] = fc[...].astype(BF16)


def finish_states(a1, states):
    for h in range(HEADS):
        pieces = [a1[holder(h, jg)].astype(F32) for jg in range(JG)]
        for s in range(2):
            states[s, h] = jnp.concatenate([p[s * JW : (s + 1) * JW] for p in pieces], axis=0).T


def remote(axis, peer, src, dst, sems, n):
    return pltpu.make_async_remote_copy(
        src_ref=src,
        dst_ref=dst,
        send_sem=sems.at[0, n],
        recv_sem=sems.at[1, n],
        device_id={axis: peer},
        device_id_type=pl.DeviceIdType.MESH,
    )


def whole(
    columns,
    states_in,
    conv_in,
    proj_in,
    taps_in,
    decay_in,
    rate_in,
    beta_in,
    gate_in,
    gain_in,
    weight_in,
    targets_in,
    live_in,
    out_to,
    states_to,
    conv_to,
    states,
    conv,
    proj,
    taps,
    decay,
    rate,
    beta,
    gate,
    gain,
    weight,
    targets,
    live,
    out,
    conv_out,
    s1,
    s2,
    s3,
    r1,
    r2,
    r3,
    b1,
    b2,
    a1,
    a2,
    partial,
    shares,
    f,
    f1,
    f2,
    mem,
    places,
    xt,
    fc,
    fg,
    local,
    sems,
):
    me = lax.axis_index("rep")
    col = lax.axis_index("head")
    z, x, core = me // (XS * CS), (me // CS) % XS, me % CS
    mine = (core * XS + x) * ZS + z
    head, jg = z % HEADS, (z // HEADS) * 8 + core * XS + x

    barrier = pltpu.get_barrier_semaphore()

    def greet(k, _):
        pl.semaphore_signal(
            barrier,
            inc=1,
            device_id={"rep": lax.rem(me + k, GROUPS)},
            device_id_type=pl.DeviceIdType.MESH,
        )
        return 0

    lax.fori_loop(1, GROUPS, greet, 0)
    for k in range(1, columns):
        pl.semaphore_signal(
            barrier,
            inc=1,
            device_id={"head": lax.rem(col + k, columns)},
            device_id_type=pl.DeviceIdType.MESH,
        )

    loads = [
        pltpu.make_async_copy(src, dst, local.at[n])
        for n, (src, dst) in enumerate(
            [
                (conv_in, conv),
                (proj_in, proj),
                (decay_in, decay),
                (beta_in, beta),
                (live_in, live),
                (states_in, states),
                (targets_in, targets),
                (taps_in, taps),
                (rate_in, rate),
                (gate_in, gate),
                (gain_in, gain),
                (weight_in, weight),
            ]
        )
    ]
    for load in loads:
        load.start()
    for load in loads[:3]:
        load.wait()
    pack_inputs(conv, proj, decay, s2, f)
    pl.semaphore_wait(barrier, GROUPS - 1 + columns - 1)

    keep = pltpu.make_async_copy(s2.at[head], r2.at[core, x, z], local.at[12])
    keep.start()
    for k in (4, 3, 5, 2, 6, 1, 7):
        to = lax.rem(z + k, ZS)
        peer = (to * XS + x) * CS + core
        remote("rep", peer, s2.at[lax.rem(to, HEADS)], r2.at[core, x, z], sems, 0).start()

    for load in loads[3:6]:
        load.wait()
    pack_values(conv, proj, beta, live, s3)
    pack_states(states, s1)

    keep.wait()
    done = remote("rep", me, r2.at[0, 0, pl.ds(0, ZS - 1)], r2.at[0, 0, pl.ds(0, ZS - 1)], sems, 0)
    done.wait_send()
    done.wait_recv()
    across = []
    for k in (2, 1, 3):
        to = lax.rem(x + k, XS)
        across.append(
            remote("rep", (z * XS + to) * CS + core, r2.at[core, x], r2.at[core, x], sems, k)
        )
        across[-1].start()
    other = me + 1 - 2 * core
    remote("rep", other, r2.at[core, x], r2.at[core, x], sems, 4).start()

    keep = [
        pltpu.make_async_copy(s1.at[mine], r1.at[mine], local.at[13]),
        pltpu.make_async_copy(s3.at[mine], r3.at[mine], local.at[14]),
    ]
    for copy in keep:
        copy.start()

    def to_all(pairs):
        def one(p):
            at = ((p % CS) * XS + (p // CS) % XS) * ZS + p // (XS * CS)
            for src, dst, n in pairs:
                remote("rep", p, src.at[at], dst.at[mine], sems, n).start()

        def send(i, _):
            one(lax.rem(me + 31 - i, GROUPS))
            one(lax.rem(me + GROUPS - 31 + i, GROUPS))
            return 0

        one(lax.rem(me + GROUPS // 2, GROUPS))
        lax.fori_loop(0, GROUPS // 2 - 1, send, 0)

    def from_all(dst, n):
        most = dst.at[pl.ds(0, GROUPS - 1)]
        done = remote("rep", me, most, most, sems, n)
        done.wait_send()
        done.wait_recv()

    to_all([(s3, r3, 5), (s1, r1, 6)])

    widen_inputs(r2, f2, core, x)
    for load in loads[6:9]:
        load.wait()
    find_places(targets, places)
    for n, k in enumerate((2, 1, 3)):
        origin = lax.rem(x + XS - k, XS)
        across[n].wait_recv()
        remote("rep", other, r2.at[core, origin], r2.at[core, origin], sems, 4).start()
        widen_inputs(r2, f2, core, origin)
    for copy in keep:
        copy.wait()
    from_all(r1, 6)
    enter_states(r1, f1, mem)
    for copy in across:
        copy.wait_send()
    done = remote("rep", me, r2.at[0], r2.at[0], sems, 4)
    done.wait_send()
    done.wait_recv()
    for n in range(XS):
        widen_inputs(r2, f2, 1 - core, n)
    from_all(r3, 5)

    rate_here = jnp.sum(
        jnp.where(iota((1, HEADS), 1) == head, rate[...], 0.0), axis=1, keepdims=True
    )
    cols = pl.ds(pl.multiple_of(head * DK, DK), DK)
    returned = run_steps(jg, f2, r3, taps.at[:, :, cols], rate_here, places, mem, xt)
    for s in range(2):
        b2[:, s, :] = returned[s * GROUPS : (s + 1) * GROUPS]
    keep = pltpu.make_async_copy(b2.at[mine], a2.at[mine], local.at[12])
    keep.start()
    to_all([(b2, a2, 7)])
    leave_states(places[STEPS - 1], mem, f1, b1)
    keep_states = pltpu.make_async_copy(b1.at[mine], a1.at[mine], local.at[13])
    keep_states.start()
    to_all([(b1, a1, 8)])

    for load in loads[9:]:
        load.wait()
    keep.wait()
    from_all(a2, 7)
    finish_rows(a2, gate, gain, live, weight, conv_out, partial, fc, fg)
    keep = pltpu.make_async_copy(partial.at[col], shares.at[col], local.at[12])
    keep.start()
    for k in (4, 3, 5, 2, 6, 1, 7):
        to = lax.rem(col + k, columns)
        remote("head", to, partial.at[to], shares.at[col], sems, 9).start()
    stores = [pltpu.make_async_copy(conv_out, conv_to, local.at[14])]
    stores[0].start()

    keep_states.wait()
    from_all(a1, 8)
    finish_states(a1, states)
    stores.append(pltpu.make_async_copy(states, states_to, local.at[13]))
    stores[1].start()

    keep.wait()
    most = shares.at[pl.ds(0, columns - 1)]
    done = remote("head", col, most, most, sems, 9)
    done.wait_send()
    done.wait_recv()
    total = shares[0].astype(F32)
    for n in range(1, columns):
        total = total + shares[n].astype(F32)
    for t in range(STEPS):
        out[t] = total[2 * t : 2 * t + 2, : out.shape[2]].astype(BF16)
    stores.append(pltpu.make_async_copy(out, out_to, local.at[12]))
    stores[2].start()
    for store in stores:
        store.wait()


def shape(dims, kind):
    return jax.ShapeDtypeStruct(dims, kind)


def local(columns, *args):
    (
        states,
        conv_states,
        projected,
        conv_weight,
        decay_input,
        decay_rate,
        beta_logit,
        out_gate,
        norm_gain,
        out_weight,
        destinations,
        live_counts,
    ) = args
    operands = (
        states,
        conv_states.transpose(1, 2, 0, 3),
        projected.transpose(0, 2, 1, 3),
        conv_weight.transpose(1, 0, 2),
        decay_input,
        decay_rate.reshape(1, HEADS),
        beta_logit.transpose(1, 2, 0),
        out_gate,
        norm_gain.reshape(1, DK),
        out_weight,
        destinations,
        live_counts.transpose(1, 0),
    )
    share = out_weight.shape[1] // columns
    width = -(-share // DK) * DK
    block = pltpu.VMEM((GROUPS, 16, DK), BF16)
    small = pltpu.VMEM((GROUPS, 2, DK), F32)
    any_ = pl.BlockSpec(memory_space=pl.ANY)
    out, states_out, conv_out = pl.pallas_call(
        functools.partial(whole, columns),
        out_shape=(
            shape((STEPS, 2, share), BF16),
            shape(states.shape, F32),
            shape(operands[1].shape, BF16),
        ),
        in_specs=[any_] * len(operands),
        out_specs=(any_,) * 3,
        scratch_shapes=[pltpu.VMEM(a.shape, a.dtype) for a in operands]
        + [
            pltpu.VMEM((STEPS, 2, share), BF16),
            pltpu.VMEM(operands[1].shape, BF16),
            block,
            pltpu.VMEM((HEADS, ROWS, DK), BF16),
            small,
            block,
            pltpu.VMEM((CS, XS, ZS, ROWS, DK), BF16),
            small,
            block,
            small,
            block,
            small,
            pltpu.VMEM((columns, 16, width), BF16),
            pltpu.VMEM((columns, 16, width), BF16),
            pltpu.VMEM((HEADS, ROWS, DK), F32),
            pltpu.VMEM((GROUPS * 16, DK), F32),
            pltpu.VMEM((GROUPS * ROWS, DK), F32),
            pltpu.VMEM((JW, DK, SLOTS), F32),
            pltpu.VMEM((STEPS, SLOTS, SLOTS), BF16),
            pltpu.VMEM((DK, SLOTS), F32),
            pltpu.VMEM(operands[1].shape, F32),
            pltpu.VMEM((16, HEADS * DK), F32),
            pltpu.SemaphoreType.DMA((15,)),
            pltpu.SemaphoreType.DMA((2, 10)),
        ],
        compiler_params=pltpu.CompilerParams(
            collective_id=0, has_side_effects=True, vmem_limit_bytes=48 * 1024 * 1024
        ),
        name="kda_steps",
    )(*operands)
    return out, states_out, conv_out.transpose(2, 0, 1, 3)


def solution(mesh):
    placed = (
        P("rep", "head", None, None),
        P("rep", None, None, "head"),
        P(None, "rep", None, "head"),
        P(None, None, "head"),
        P(None, "rep", "head"),
        P("head"),
        P(None, "rep", "head"),
        P(None, "rep", "head"),
        P(),
        P("head", None),
        P(),
        P(None, "rep"),
    )
    return jax.shard_map(
        functools.partial(local, mesh.shape["head"]),
        mesh=mesh,
        in_specs=placed,
        out_specs=(
            P(None, "rep", "head"),
            P("rep", "head", None, None),
            P("rep", None, None, "head"),
        ),
        check_vma=False,
    )
```

time: 919 us -> 63.9 us (0.07); the launches traced: 902 us -> 63.3 us
  waiting for transfers between devices: 408 us -> 0 us
  starting transfers between devices: 200 us -> 0 us
  local copies, waits for them, and re-layouts: 173 us -> 11.7 us
  other arithmetic: 91.2 us -> 0 us
  Pallas kernels: 0 us -> 50.9 us
  between operations: 16.1 us -> 0.66 us
  matrix products: 13.3 us -> 0 us
    unnamed x12 -> x0, waiting for transfers between devices: 207 us -> none
    all_to_all x24 -> x0, waiting for transfers between devices: 201 us -> none  [the longest x6 101 us: move_every(): lax.all_to_all(history.astype(jnp.float32), 'rep', split_axis=2, concat_a...]
    all_to_all x24 -> x0, starting transfers between devices: 200 us -> none  [the longest x6 56.9 us: move_every(): lax.all_to_all(spread_memory[source], 'rep', split_axis=0, concat_axis=2,...]
    pallas_call x0 -> x1, Pallas kernels: none -> 50.9 us  [local(): pl.pallas_call(functools.partial(whole, columns), out_shape=(shape((STEPS...]
    reduce_sum x30 -> x0, other arithmetic: 41.3 us -> none  [the longest x6 18 us: layer_step(): readout = jnp.sum(query[..., None] * updated, axis=2) * key_dim ** (-0.5)]
    all_to_all x47 -> x0, local copies, waits for them, and re-layouts: 31.4 us -> none  [the longest x17 11.7 us: move_every(): lax.all_to_all(memory, 'rep', split_axis=2, concat_axis=0, tiled=True)]
    div x12 -> x0, local copies, waits for them, and re-layouts: 28.6 us -> none  [unit_rows(): vectors / jnp.sqrt(jnp.sum(vectors * vectors, axis=-1, keepdims=True) + E...]
    gather x12 -> x0, local copies, waits for them, and re-layouts: 21.5 us -> none  [the longest x6 12.7 us: move_every(): spread_memory[source]]
  transfers between devices with their start and end apart: 30 -> 0, of which waited for: 22 -> 0; matrix products, arithmetic and copies ran while one was open for 22% -> 0% of each run, Pallas kernels for 0% -> 0%
where the time goes in v2:
time: 63.9 us; the launch traced here: 63.3 us
  Pallas kernels  50.9 us (80%)
  local copies, waits for them, and re-layouts  11.7 us (18%)
  between operations  0.66 us (1%)
    pallas_call x1, Pallas kernels, local(): pl.pallas_call(functools.partial(whole, columns), out_shape=(shape((STEPS...  50.9 us
    unnamed x27, local copies, waits for them, and re-layouts  11.7 us

profile of v2, /device:TPU:1, one launch (start us, length us, event | category | flops | bytes accessed | tf_op | source)
XLA Modules:
  0.0 63.3 jit_solution(1728030334347551331)
XLA Ops:
  0.6 0.0 copy-start
  0.6 1.7 %copy-done = bf16[512,2304]{1,0:T(8,128)(2,1)S(1)} copy-done((bf16[512,2304]{1,0:T(8,128)(2,1)S(1)}, bf16[512,2304]{1,0:T(8,128)(2,1)}, u32[]{:S(2)}) %copy-start) | copy-done | bytes 2359320
  2.3 0.0 copy-start.1
  2.3 1.0 %copy-done.1 = f32[2,4,128,128]{3,2,1,0:T(8,128)S(1)} copy-done((f32[2,4,128,128]{3,2,1,0:T(8,128)S(1)}, f32[2,4,128,128]{3,2,1,0:T(8,128)}, u32[]{:S(2)}) %copy-start.1) | copy-done | bytes 524312
  3.3 0.0 copy-start.2
  3.3 0.8 %copy-done.2 = bf16[6,2,3,512]{3,1,2,0:T(2,128)(2,1)S(1)} copy-done((bf16[6,2,3,512]{3,1,2,0:T(2,128)(2,1)S(1)}, bf16[6,2,3,512]{3,1,2,0:T(2,128)(2,1)}, u32[]{:S(2)}) %copy-start.2) | copy-done | bytes 36888
  4.1 0.0 copy-start.3
  4.1 0.7 %copy-done.3 = f32[4,3,512]{2,0,1:T(4,128)S(1)} copy-done((f32[4,3,512]{2,0,1:T(4,128)S(1)}, f32[4,3,512]{2,0,1:T(4,128)}, u32[]{:S(2)}) %copy-start.3) | copy-done | bytes 24600
  4.8 0.0 copy-start.4
  4.9 0.7 %copy-done.4 = f32[6,2,512]{2,1,0:T(2,128)S(1)} copy-done((f32[6,2,512]{2,1,0:T(2,128)S(1)}, f32[6,2,512]{2,1,0:T(2,128)}, u32[]{:S(2)}) %copy-start.4) | copy-done | bytes 24600
  5.6 0.0 copy-start.5
  5.6 0.7 %copy-done.5 = bf16[2,3,3,512]{3,0,2,1:T(2,128)(2,1)S(1)} copy-done((bf16[2,3,3,512]{3,0,2,1:T(2,128)(2,1)S(1)}, bf16[2,3,3,512]{3,0,2,1:T(2,128)(2,1)}, u32[]{:S(2)}) %copy-start.5) | copy-done | bytes 18456
  6.3 0.0 copy-start.6
  6.3 0.7 %copy-done.6 = bf16[6,2,512]{2,1,0:T(2,128)(2,1)S(1)} copy-done((bf16[6,2,512]{2,1,0:T(2,128)(2,1)S(1)}, bf16[6,2,512]{2,1,0:T(2,128)(2,1)}, u32[]{:S(2)}) %copy-start.6) | copy-done | bytes 12312
  7.0 0.0 copy-start.7
  7.0 0.7 %copy-done.7 = f32[6,2,4]{0,2,1:T(4,128)S(1)} copy-done((f32[6,2,4]{0,2,1:T(4,128)S(1)}, f32[6,2,4]{0,2,1:T(4,128)}, u32[]{:S(2)}) %copy-start.7) | copy-done | bytes 216
  7.7 0.0 copy-start.8
  7.7 0.7 %copy-done.8 = s32[6,128]{1,0:T(8,128)S(1)} copy-done((s32[6,128]{1,0:T(8,128)S(1)}, s32[6,128]{1,0:T(8,128)}, u32[]{:S(2)}) %copy-start.8) | copy-done | bytes 3096
  8.4 0.0 copy-start.9
  8.4 0.7 %copy-done.9 = f32[4]{0:T(128)S(1)} copy-done((f32[4]{0:T(128)S(1)}, f32[4]{0:T(128)}, u32[]{:S(2)}) %copy-start.9) | copy-done | bytes 40
  9.0 0.0 copy-start.10
  9.1 0.7 %copy-done.10 = f32[128]{0:T(128)S(1)} copy-done((f32[128]{0:T(128)S(1)}, f32[128]{0:T(128)}, u32[]{:S(2)}) %copy-start.10) | copy-done | bytes 536
  9.7 0.0 copy-start.11
  9.7 0.7 %copy-done.11 = s32[6,1]{0,1:T(1,128)S(1)} copy-done((s32[6,1]{0,1:T(1,128)S(1)}, s32[6,1]{0,1:T(1,128)}, u32[]{:S(2)}) %copy-start.11) | copy-done | bytes 48
  10.4 50.9 %kda_steps.1 = (bf16[6,2,288]{2,1,0:T(2,128)(2,1)S(1)}, f32[2,4,128,128]{3,2,1,0:T(8,128)S(1)}, bf16[3,3,2,512]{3,2,1,0:T(2,128)(2,1)S(1)}) custom-call(f32[2,4,128,128]{3,2,1,0:T(8,128)S(1)} %copy-done.1, bf16[3,3,2,512]{3,2,1,0:T(2,128)(2,1)S(1)} %bitcast.11, bf16[6,3,2,512]{3,2,1,0:T(2,128)(2,1)S(1)} %bitcast.8, f32[3,4,512]{2,1,0:T(4,128)S(1)} %bitcast.9, ...), custom_call_target="tpu_custom_call" | custom-call | tf_op jit(solution)/shard_map/kda_steps/pallas_call | solution.py:579
  61.3 0.6 copy.18
  61.9 0.8 %copy.19 = f32[2,4,128,128]{3,2,1,0:T(8,128)} copy(f32[2,4,128,128]{3,2,1,0:T(8,128)S(1)} %get-tuple-element.13) | data formatting | bytes 1048576
  62.7 0.6 copy.20
Async XLA Ops:
  0.6 1.7 %copy-start = (bf16[512,2304]{1,0:T(8,128)(2,1)S(1)}, bf16[512,2304]{1,0:T(8,128)(2,1)}, u32[]{:S(2)}) copy-start(bf16[512,2304]{1,0:T(8,128)(2,1)} %weight_in.1) | copy-start | bytes 7077892
  2.3 1.0 %copy-start.1 = (f32[2,4,128,128]{3,2,1,0:T(8,128)S(1)}, f32[2,4,128,128]{3,2,1,0:T(8,128)}, u32[]{:S(2)}) copy-start(f32[2,4,128,128]{3,2,1,0:T(8,128)} %states_in.1) | copy-start | bytes 1572868
  3.3 0.8 %copy-start.2 = (bf16[6,2,3,512]{3,1,2,0:T(2,128)(2,1)S(1)}, bf16[6,2,3,512]{3,1,2,0:T(2,128)(2,1)}, u32[]{:S(2)}) copy-start(bf16[6,2,3,512]{3,1,2,0:T(2,128)(2,1)} %param.14) | copy-start | bytes 110596
  4.1 0.7 %copy-start.3 = (f32[4,3,512]{2,0,1:T(4,128)S(1)}, f32[4,3,512]{2,0,1:T(4,128)}, u32[]{:S(2)}) copy-start(f32[4,3,512]{2,0,1:T(4,128)} %param.15) | copy-start | bytes 73732
  4.8 0.7 %copy-start.4 = (f32[6,2,512]{2,1,0:T(2,128)S(1)}, f32[6,2,512]{2,1,0:T(2,128)}, u32[]{:S(2)}) copy-start(f32[6,2,512]{2,1,0:T(2,128)} %decay_in.1) | copy-start | bytes 73732
  5.6 0.7 %copy-start.5 = (bf16[2,3,3,512]{3,0,2,1:T(2,128)(2,1)S(1)}, bf16[2,3,3,512]{3,0,2,1:T(2,128)(2,1)}, u32[]{:S(2)}) copy-start(bf16[2,3,3,512]{3,0,2,1:T(2,128)(2,1)} %param.13) | copy-start | bytes 55300
  6.3 0.7 %copy-start.6 = (bf16[6,2,512]{2,1,0:T(2,128)(2,1)S(1)}, bf16[6,2,512]{2,1,0:T(2,128)(2,1)}, u32[]{:S(2)}) copy-start(bf16[6,2,512]{2,1,0:T(2,128)(2,1)} %gate_in.1) | copy-start | bytes 36868
  7.0 0.7 %copy-start.7 = (f32[6,2,4]{0,2,1:T(4,128)S(1)}, f32[6,2,4]{0,2,1:T(4,128)}, u32[]{:S(2)}) copy-start(f32[6,2,4]{0,2,1:T(4,128)} %param.18) | copy-start | bytes 580
  7.7 0.7 %copy-start.8 = (s32[6,128]{1,0:T(8,128)S(1)}, s32[6,128]{1,0:T(8,128)}, u32[]{:S(2)}) copy-start(s32[6,128]{1,0:T(8,128)} %targets_in.1) | copy-start | bytes 9220
  8.4 0.7 %copy-start.9 = (f32[4]{0:T(128)S(1)}, f32[4]{0:T(128)}, u32[]{:S(2)}) copy-start(f32[4]{0:T(128)} %param.17) | copy-start | bytes 52
  9.0 0.7 %copy-start.10 = (f32[128]{0:T(128)S(1)}, f32[128]{0:T(128)}, u32[]{:S(2)}) copy-start(f32[128]{0:T(128)} %param.20) | copy-start | bytes 1540
  9.7 0.7 %copy-start.11 = (s32[6,1]{0,1:T(1,128)S(1)}, s32[6,1]{0,1:T(1,128)}, u32[]{:S(2)}) copy-start(s32[6,1]{0,1:T(1,128)} %param.23) | copy-start | bytes 76

commit v3 on v2

--- a/solution.py
+++ b/solution.py
@@ -15,9 +15,8 @@
 SLOTS = 2 * GROUPS
 JG, JW = 16, 8
 WIN = HIST + STEPS
-ROW_HI = WIN * 4
-ROW_LO = ROW_HI + 2 * STEPS
-ROWS = 64
+ROW_DECAY = WIN * 4
+ROWS = ROW_DECAY + 2 * STEPS
 LANE_ALIVE = WIN * JW
 LANE_BETA = LANE_ALIVE + 8
 CONV = 3 * HIST
@@ -68,7 +67,7 @@
     ]
 
 
-def pack_inputs(conv, proj, decay, s2, f):
+def pack_inputs(conv, proj, decay, rate, s2, f):
     for w in range(WIN):
         for part in range(2):
             block = (conv[w, part] if w < HIST else proj[w - HIST, part]).astype(F32)
@@ -76,14 +75,11 @@
             for h in range(HEADS):
                 f[h, at : at + 2, :] = block[:, h * DK : (h + 1) * DK]
     for t in range(STEPS):
-        lead, rest = halves(decay[t])
-        lead, rest = lead.astype(F32), rest.astype(F32)
+        exponent = softplus(decay[t])
         for h in range(HEADS):
-            cols = slice(h * DK, (h + 1) * DK)
-            f[h, ROW_HI + 2 * t : ROW_HI + 2 * t + 2, :] = lead[:, cols]
-            f[h, ROW_LO + 2 * t : ROW_LO + 2 * t + 2, :] = rest[:, cols]
+            at = ROW_DECAY + 2 * t
+            f[h, at : at + 2, :] = exponent[:, h * DK : (h + 1) * DK] * rate[0:1, h : h + 1]
     for h in range(HEADS):
-        f[h, ROW_LO + 2 * STEPS : ROWS, :] = jnp.zeros((ROWS - ROW_LO - 2 * STEPS, DK), F32)
         s2[h] = f[h].astype(BF16)
 
 
@@ -123,13 +119,13 @@
             s1[holder(h, jg)] = jnp.concatenate([first[rows], second[rows]], axis=0).astype(BF16)
 
 
-def widen_inputs(r2, f2, core, x):
+def widen_inputs(r2, f2, core, x, first, last):
     def one(i, _):
         at = pl.multiple_of(((core * XS + x) * ZS + i) * ROWS, ROWS)
         f2[pl.ds(at, ROWS), :] = r2[core, x, i].astype(F32)
         return 0
 
-    lax.fori_loop(0, ZS, one, 0)
+    lax.fori_loop(first, last, one, 0)
 
 
 def enter_states(r1, f1, mem):
@@ -155,7 +151,7 @@
             held = contract(back, place, 1, 0).astype(BF16)
 
 
-def run_steps(jg, f2, r3, weight, rate, places, mem, xt):
+def run_steps(jg, f2, r3, weight, places, mem, xt):
     def both(row):
         return jnp.concatenate(
             [f2[pl.ds(row + s, GROUPS, stride=ROWS), :] for s in range(2)], axis=0
@@ -182,14 +178,13 @@
     readouts = []
     for t in range(STEPS):
         place = places[t]
-        four = pair(t + HIST, [both(ROW_HI + 2 * t), both(ROW_LO + 2 * t)], place)
-        decay = four[2 * DK : 3 * DK] + four[3 * DK :]
+        three = pair(t + HIST, [both(ROW_DECAY + 2 * t)], place)
         small = contract(lead3, place, 0, 0) + contract(rest3, place, 0, 0)
-        new = [four[:DK], four[DK : 2 * DK], small[(t + HIST) * JW : (t + HIST + 1) * JW]]
+        new = [three[:DK], three[DK : 2 * DK], small[(t + HIST) * JW : (t + HIST + 1) * JW]]
         alive = small[LANE_ALIVE + t : LANE_ALIVE + t + 1] > 0.5
         logit = small[LANE_BETA + t : LANE_BETA + t + 1]
         strength = jnp.where(alive, sigmoid(logit), 0.0)
-        retain = jnp.where(alive, jnp.exp(-rate * softplus(decay)), 1.0)
+        retain = jnp.where(alive, jnp.exp(-three[2 * DK :]), 1.0)
         window = hist + [new]
         acts = []
         for part in range(3):
@@ -392,12 +387,12 @@
                 (conv_in, conv),
                 (proj_in, proj),
                 (decay_in, decay),
+                (rate_in, rate),
                 (beta_in, beta),
                 (live_in, live),
                 (states_in, states),
                 (targets_in, targets),
                 (taps_in, taps),
-                (rate_in, rate),
                 (gate_in, gate),
                 (gain_in, gain),
                 (weight_in, weight),
@@ -406,9 +401,9 @@
     ]
     for load in loads:
         load.start()
-    for load in loads[:3]:
+    for load in loads[:4]:
         load.wait()
-    pack_inputs(conv, proj, decay, s2, f)
+    pack_inputs(conv, proj, decay, rate, s2, f)
     pl.semaphore_wait(barrier, GROUPS - 1 + columns - 1)
 
     keep = pltpu.make_async_copy(s2.at[head], r2.at[core, x, z], local.at[12])
@@ -418,7 +413,7 @@
         peer = (to * XS + x) * CS + core
         remote("rep", peer, s2.at[lax.rem(to, HEADS)], r2.at[core, x, z], sems, 0).start()
 
-    for load in loads[3:6]:
+    for load in loads[4:7]:
         load.wait()
     pack_values(conv, proj, beta, live, s3)
     pack_states(states, s1)
@@ -427,15 +422,27 @@
     done = remote("rep", me, r2.at[0, 0, pl.ds(0, ZS - 1)], r2.at[0, 0, pl.ds(0, ZS - 1)], sems, 0)
     done.wait_send()
     done.wait_recv()
-    across = []
-    for k in (2, 1, 3):
-        to = lax.rem(x + k, XS)
-        across.append(
-            remote("rep", (z * XS + to) * CS + core, r2.at[core, x], r2.at[core, x], sems, k)
-        )
-        across[-1].start()
+    right = (z * XS + lax.rem(x + 1, XS)) * CS + core
+    left = (z * XS + lax.rem(x + XS - 1, XS)) * CS + core
     other = me + 1 - 2 * core
-    remote("rep", other, r2.at[core, x], r2.at[core, x], sems, 4).start()
+    half = ZS // 2
+    behind, ahead = lax.rem(x + XS - 1, XS), lax.rem(x + 1, XS)
+
+    def part(origin, n):
+        return r2.at[core, origin, pl.ds(n * half, half)]
+
+    def pass_on(peer, origin, n, sem):
+        copy = remote("rep", peer, part(origin, n), part(origin, n), sems, sem)
+        copy.start()
+        return copy
+
+    ring = [
+        pass_on(right, x, 0, 1),
+        pass_on(left, x, 1, 2),
+        pass_on(right, x, 1, 3),
+        pass_on(left, x, 0, 4),
+    ]
+    remote("rep", other, r2.at[core, x], r2.at[core, x], sems, 10).start()
 
     keep = [
         pltpu.make_async_copy(s1.at[mine], r1.at[mine], local.at[13]),
@@ -466,33 +473,44 @@
 
     to_all([(s3, r3, 5), (s1, r1, 6)])
 
-    widen_inputs(r2, f2, core, x)
-    for load in loads[6:9]:
+    widen_inputs(r2, f2, core, x, 0, ZS)
+
+    def arrived(copy, origin, n):
+        copy.wait_recv()
+        pass_on(other, origin, n, 10)
+        widen_inputs(r2, f2, core, origin, n * half, (n + 1) * half)
+
+    ring[0].wait_recv()
+    ring.append(pass_on(right, behind, 0, 11))
+    pass_on(other, behind, 0, 10)
+    ring[1].wait_recv()
+    ring.append(pass_on(left, ahead, 1, 12))
+    pass_on(other, ahead, 1, 10)
+    for load in loads[7:9]:
         load.wait()
     find_places(targets, places)
-    for n, k in enumerate((2, 1, 3)):
-        origin = lax.rem(x + XS - k, XS)
-        across[n].wait_recv()
-        remote("rep", other, r2.at[core, origin], r2.at[core, origin], sems, 4).start()
-        widen_inputs(r2, f2, core, origin)
+    widen_inputs(r2, f2, core, behind, 0, half)
+    widen_inputs(r2, f2, core, ahead, half, ZS)
+    arrived(ring[2], behind, 1)
+    arrived(ring[3], ahead, 0)
+    opposite = lax.rem(x + 2, XS)
+    arrived(ring[4], opposite, 0)
+    arrived(ring[5], opposite, 1)
     for copy in keep:
         copy.wait()
     from_all(r1, 6)
     enter_states(r1, f1, mem)
-    for copy in across:
+    for copy in ring:
         copy.wait_send()
-    done = remote("rep", me, r2.at[0], r2.at[0], sems, 4)
+    done = remote("rep", me, r2.at[0], r2.at[0], sems, 10)
     done.wait_send()
     done.wait_recv()
     for n in range(XS):
-        widen_inputs(r2, f2, 1 - core, n)
+        widen_inputs(r2, f2, 1 - core, n, 0, ZS)
     from_all(r3, 5)
 
-    rate_here = jnp.sum(
-        jnp.where(iota((1, HEADS), 1) == head, rate[...], 0.0), axis=1, keepdims=True
-    )
     cols = pl.ds(pl.multiple_of(head * DK, DK), DK)
-    returned = run_steps(jg, f2, r3, taps.at[:, :, cols], rate_here, places, mem, xt)
+    returned = run_steps(jg, f2, r3, taps.at[:, :, cols], places, mem, xt)
     for s in range(2):
         b2[:, s, :] = returned[s * GROUPS : (s + 1) * GROUPS]
     keep = pltpu.make_async_copy(b2.at[mine], a2.at[mine], local.at[12])
@@ -575,7 +593,7 @@
     width = -(-share // DK) * DK
     block = pltpu.VMEM((GROUPS, 16, DK), BF16)
     small = pltpu.VMEM((GROUPS, 2, DK), F32)
-    any_ = pl.BlockSpec(memory_space=pl.ANY)
+    any_ = pl.BlockSpec(memory_space=pltpu.HBM)
     out, states_out, conv_out = pl.pallas_call(
         functools.partial(whole, columns),
         out_shape=(
@@ -610,10 +628,10 @@
             pltpu.VMEM(operands[1].shape, F32),
             pltpu.VMEM((16, HEADS * DK), F32),
             pltpu.SemaphoreType.DMA((15,)),
-            pltpu.SemaphoreType.DMA((2, 10)),
+            pltpu.SemaphoreType.DMA((2, 13)),
         ],
         compiler_params=pltpu.CompilerParams(
-            collective_id=0, has_side_effects=True, vmem_limit_bytes=48 * 1024 * 1024
+            collective_id=0, has_side_effects=True, vmem_limit_bytes=60 * 1024 * 1024
         ),
         name="kda_steps",
     )(*operands)

time: 63.9 us -> 54.3 us (0.85)
  local copies, waits for them, and re-layouts: 11.7 us -> 4.52 us
  Pallas kernels: 50.9 us -> 48.8 us
    unnamed x27 -> x3, local copies, waits for them, and re-layouts: 11.7 us -> 4.52 us
    pallas_call x1, Pallas kernels: 50.9 us -> 48.8 us  [local(): pl.pallas_call(functools.partial(whole, columns), out_shape=(shape((STEPS...]
where the time goes in v3:
time: 54.3 us; the launch traced here: 54 us
  Pallas kernels  48.8 us (90%)
  local copies, waits for them, and re-layouts  4.52 us (8%)
  between operations  0.64 us (1%)
    pallas_call x1, Pallas kernels, local(): pl.pallas_call(functools.partial(whole, columns), out_shape=(shape((STEPS...  48.8 us
    unnamed x3, local copies, waits for them, and re-layouts  4.52 us

profile of v3, /device:TPU:1, one launch (start us, length us, event | category | flops | bytes accessed | tf_op | source)
XLA Modules:
  0.0 54.0 jit_solution(5707228517617725524)
XLA Ops:
  0.6 48.8 %kda_steps.1 = (bf16[6,2,288]{2,1,0:T(2,128)(2,1)}, f32[2,4,128,128]{3,2,1,0:T(8,128)}, bf16[3,3,2,512]{3,2,1,0:T(2,128)(2,1)}) custom-call(f32[2,4,128,128]{3,2,1,0:T(8,128)} %states_in.1, bf16[3,3,2,512]{3,2,1,0:T(2,128)(2,1)} %bitcast.11, bf16[6,3,2,512]{3,2,1,0:T(2,128)(2,1)} %bitcast.8, f32[3,4,512]{2,1,0:T(4,128)} %bitcast.9, f32[6,2,512]{2,1,0:T(2,128)} %decay_in.1, ...), custom_call_target="tpu_custom_call" | custom-call | tf_op jit(solution)/shard_map/kda_steps/pallas_call | solution.py:597
  49.5 1.3 %copy.18 = bf16[6,2,288]{2,1,0:T(2,128)(2,1)} copy(bf16[6,2,288]{2,1,0:T(2,128)(2,1)} %get-tuple-element.12) | data formatting | bytes 13824
  50.8 1.9 %copy.19 = f32[2,4,128,128]{3,2,1,0:T(8,128)} copy(f32[2,4,128,128]{3,2,1,0:T(8,128)} %get-tuple-element.13) | data formatting | bytes 1048576
  52.6 1.3 %copy.20 = bf16[2,3,3,512]{3,0,2,1:T(2,128)(2,1)} copy(bf16[2,3,3,512]{3,0,2,1:T(2,128)(2,1)} %bitcast.10) | data formatting | bytes 36864

commit v4 on v3

--- a/solution.py
+++ b/solution.py
@@ -282,13 +282,6 @@
     conv[...] = fc[...].astype(BF16)
 
 
-def finish_states(a1, states):
-    for h in range(HEADS):
-        pieces = [a1[holder(h, jg)].astype(F32) for jg in range(JG)]
-        for s in range(2):
-            states[s, h] = jnp.concatenate([p[s * JW : (s + 1) * JW] for p in pieces], axis=0).T
-
-
 def remote(axis, peer, src, dst, sems, n):
     return pltpu.make_async_remote_copy(
         src_ref=src,
@@ -298,6 +291,17 @@
         device_id={axis: peer},
         device_id_type=pl.DeviceIdType.MESH,
     )
+
+
+def peers_far_first(me, act):
+    act(lax.rem(me + GROUPS // 2, GROUPS))
+
+    def two(i, _):
+        act(lax.rem(me + 31 - i, GROUPS))
+        act(lax.rem(me + GROUPS - 31 + i, GROUPS))
+        return 0
+
+    lax.fori_loop(0, GROUPS // 2 - 1, two, 0)
 
 
 def whole(
@@ -314,8 +318,8 @@
     weight_in,
     targets_in,
     live_in,
-    out_to,
-    states_to,
+    a1,
+    shares,
     conv_to,
     states,
     conv,
@@ -329,7 +333,6 @@
     weight,
     targets,
     live,
-    out,
     conv_out,
     s1,
     s2,
@@ -339,10 +342,8 @@
     r3,
     b1,
     b2,
-    a1,
     a2,
     partial,
-    shares,
     f,
     f1,
     f2,
@@ -362,23 +363,14 @@
 
     barrier = pltpu.get_barrier_semaphore()
 
-    def greet(k, _):
+    def greet(axis, peer):
         pl.semaphore_signal(
-            barrier,
-            inc=1,
-            device_id={"rep": lax.rem(me + k, GROUPS)},
-            device_id_type=pl.DeviceIdType.MESH,
+            barrier, inc=1, device_id={axis: peer}, device_id_type=pl.DeviceIdType.MESH
         )
-        return 0
-
-    lax.fori_loop(1, GROUPS, greet, 0)
+
+    peers_far_first(me, functools.partial(greet, "rep"))
     for k in range(1, columns):
-        pl.semaphore_signal(
-            barrier,
-            inc=1,
-            device_id={"head": lax.rem(col + k, columns)},
-            device_id_type=pl.DeviceIdType.MESH,
-        )
+        greet("head", lax.rem(col + k, columns))
 
     loads = [
         pltpu.make_async_copy(src, dst, local.at[n])
@@ -457,13 +449,7 @@
             for src, dst, n in pairs:
                 remote("rep", p, src.at[at], dst.at[mine], sems, n).start()
 
-        def send(i, _):
-            one(lax.rem(me + 31 - i, GROUPS))
-            one(lax.rem(me + GROUPS - 31 + i, GROUPS))
-            return 0
-
-        one(lax.rem(me + GROUPS // 2, GROUPS))
-        lax.fori_loop(0, GROUPS // 2 - 1, send, 0)
+        peers_far_first(me, one)
 
     def from_all(dst, n):
         most = dst.at[pl.ds(0, GROUPS - 1)]
@@ -531,27 +517,46 @@
     for k in (4, 3, 5, 2, 6, 1, 7):
         to = lax.rem(col + k, columns)
         remote("head", to, partial.at[to], shares.at[col], sems, 9).start()
-    stores = [pltpu.make_async_copy(conv_out, conv_to, local.at[14])]
-    stores[0].start()
-
+    store = pltpu.make_async_copy(conv_out, conv_to, local.at[14])
+    store.start()
     keep_states.wait()
     from_all(a1, 8)
-    finish_states(a1, states)
-    stores.append(pltpu.make_async_copy(states, states_to, local.at[13]))
-    stores[1].start()
-
     keep.wait()
     most = shares.at[pl.ds(0, columns - 1)]
     done = remote("head", col, most, most, sems, 9)
     done.wait_send()
     done.wait_recv()
+    store.wait()
+
+
+def settle(a1_in, shares_in, conv_in, out_to, states_to, conv_to, a1, shares, conv, out, states, sems):
+    loads = [
+        pltpu.make_async_copy(src, dst, sems.at[n])
+        for n, (src, dst) in enumerate([(a1_in, a1), (shares_in, shares), (conv_in, conv)])
+    ]
+    for load in loads:
+        load.start()
+    loads[2].wait()
+    stores = [pltpu.make_async_copy(conv, conv_to, sems.at[3])]
+    stores[0].start()
+    loads[0].wait()
+    for h in range(HEADS):
+        pieces = [a1[holder(h, jg)].astype(F32) for jg in range(JG)]
+        for s in range(2):
+            states[s, h] = jnp.concatenate([p[s * JW : (s + 1) * JW] for p in pieces], axis=0).T
+            store = pltpu.make_async_copy(
+                states.at[s, h], states_to.at[s, h], sems.at[4 + 2 * h + s]
+            )
+            store.start()
+            stores.append(store)
+    loads[1].wait()
     total = shares[0].astype(F32)
-    for n in range(1, columns):
+    for n in range(1, shares.shape[0]):
         total = total + shares[n].astype(F32)
     for t in range(STEPS):
         out[t] = total[2 * t : 2 * t + 2, : out.shape[2]].astype(BF16)
-    stores.append(pltpu.make_async_copy(out, out_to, local.at[12]))
-    stores[2].start()
+    stores.append(pltpu.make_async_copy(out, out_to, sems.at[4 + 2 * HEADS]))
+    stores[-1].start()
     for store in stores:
         store.wait()
 
@@ -594,18 +599,21 @@
     block = pltpu.VMEM((GROUPS, 16, DK), BF16)
     small = pltpu.VMEM((GROUPS, 2, DK), F32)
     any_ = pl.BlockSpec(memory_space=pltpu.HBM)
-    out, states_out, conv_out = pl.pallas_call(
+    most = pltpu.CompilerParams(
+        collective_id=0, has_side_effects=True, vmem_limit_bytes=60 * 1024 * 1024
+    )
+    landed = (
+        shape((GROUPS, 16, DK), BF16),
+        shape((columns, 16, width), BF16),
+        shape(operands[1].shape, BF16),
+    )
+    pieces = pl.pallas_call(
         functools.partial(whole, columns),
-        out_shape=(
-            shape((STEPS, 2, share), BF16),
-            shape(states.shape, F32),
-            shape(operands[1].shape, BF16),
-        ),
+        out_shape=landed,
         in_specs=[any_] * len(operands),
         out_specs=(any_,) * 3,
         scratch_shapes=[pltpu.VMEM(a.shape, a.dtype) for a in operands]
         + [
-            pltpu.VMEM((STEPS, 2, share), BF16),
             pltpu.VMEM(operands[1].shape, BF16),
             block,
             pltpu.VMEM((HEADS, ROWS, DK), BF16),
@@ -615,9 +623,7 @@
             small,
             block,
             small,
-            block,
             small,
-            pltpu.VMEM((columns, 16, width), BF16),
             pltpu.VMEM((columns, 16, width), BF16),
             pltpu.VMEM((HEADS, ROWS, DK), F32),
             pltpu.VMEM((GROUPS * 16, DK), F32),
@@ -630,11 +636,25 @@
             pltpu.SemaphoreType.DMA((15,)),
             pltpu.SemaphoreType.DMA((2, 13)),
         ],
-        compiler_params=pltpu.CompilerParams(
-            collective_id=0, has_side_effects=True, vmem_limit_bytes=60 * 1024 * 1024
-        ),
+        compiler_params=most,
         name="kda_steps",
     )(*operands)
+    results = (
+        shape((STEPS, 2, share), BF16),
+        shape(states.shape, F32),
+        shape(operands[1].shape, BF16),
+    )
+    out, states_out, conv_out = pl.pallas_call(
+        settle,
+        out_shape=results,
+        in_specs=[any_] * 3,
+        out_specs=(any_,) * 3,
+        scratch_shapes=[pltpu.VMEM(a.shape, a.dtype) for a in landed]
+        + [pltpu.VMEM(a.shape, a.dtype) for a in results[:2]]
+        + [pltpu.SemaphoreType.DMA((5 + 2 * HEADS,))],
+        compiler_params=pltpu.CompilerParams(vmem_limit_bytes=60 * 1024 * 1024),
+        name="settle",
+    )(*pieces)
     return out, states_out, conv_out.transpose(2, 0, 1, 3)
 
 

time: 54.3 us -> 50.2 us (0.924)
  local copies, waits for them, and re-layouts: 4.52 us -> 0 us
  Pallas kernels: 48.8 us -> 49.4 us
    unnamed x3 -> x0, local copies, waits for them, and re-layouts: 4.52 us -> none
    pallas_call x1 -> x2, Pallas kernels: 48.8 us -> 49.4 us  [the longest x1 47.4 us: local(): pl.pallas_call(functools.partial(whole, columns), out_shape=landed, in_sp...]
where the time goes in v4:
time: 50.2 us; the launch traced here: 50 us
  Pallas kernels  49.4 us (98%)
  between operations  0.64 us (1%)
    pallas_call x1, Pallas kernels, local(): pl.pallas_call(functools.partial(whole, columns), out_shape=landed, in_sp...  47.4 us
    pallas_call x1, Pallas kernels, local(): pl.pallas_call(settle, out_shape=results, in_specs=[any_] * 3, out_specs=...  1.95 us

profile of v4, /device:TPU:1, one launch (start us, length us, event | category | flops | bytes accessed | tf_op | source)
XLA Modules:
  0.0 50.0 jit_solution(14108717217396400755)
XLA Ops:
  0.6 47.4 %kda_steps.1 = (bf16[64,16,128]{2,1,0:T(8,128)(2,1)}, bf16[8,16,384]{2,1,0:T(8,128)(2,1)}, bf16[3,3,2,512]{3,2,1,0:T(2,128)(2,1)}) custom-call(f32[2,4,128,128]{3,2,1,0:T(8,128)} %states_in.1, bf16[3,3,2,512]{3,2,1,0:T(2,128)(2,1)} %bitcast.10, bf16[6,3,2,512]{3,2,1,0:T(2,128)(2,1)} %bitcast.8, f32[3,4,512]{2,1,0:T(4,128)} %bitcast.9, ...), custom_call_target="tpu_custom_call" | custom-call | tf_op jit(solution)/shard_map/kda_steps/pallas_call | solution.py:610
  48.1 1.9 %settle.1 = (bf16[6,2,288]{2,1,0:T(2,128)(2,1)}, f32[2,4,128,128]{3,2,1,0:T(8,128)}, bf16[3,3,2,512]{3,2,1,0:T(2,128)(2,1)}) custom-call(bf16[64,16,128]{2,1,0:T(8,128)(2,1)} %get-tuple-element.9.a1_in, bf16[8,16,384]{2,1,0:T(8,128)(2,1)} %get-tuple-element.10.shares_in, bf16[3,3,2,512]{3,2,1,0:T(2,128)(2,1)} %get-tuple-element.11.conv_in), custom_call_target="tpu_custom_call" | custom-call | tf_op jit(solution)/shard_map/settle/pallas_call | solution.py:647

commit v5 on v4

--- a/solution.py
+++ b/solution.py
@@ -151,7 +151,7 @@
             held = contract(back, place, 1, 0).astype(BF16)
 
 
-def run_steps(jg, f2, r3, weight, places, mem, xt):
+def prepare_steps(jg, f2, r3, weight, places, ready, rows8, xt):
     def both(row):
         return jnp.concatenate(
             [f2[pl.ds(row + s, GROUPS, stride=ROWS), :] for s in range(2)], axis=0
@@ -175,7 +175,6 @@
     for w in range(HIST):
         two = pair(w, [], eye)
         hist.append([two[:DK], two[DK:], start[w * JW : (w + 1) * JW]])
-    readouts = []
     for t in range(STEPS):
         place = places[t]
         three = pair(t + HIST, [both(ROW_DECAY + 2 * t)], place)
@@ -198,17 +197,10 @@
             for n in range(HIST)
         ]
         query, key, value = acts
-        query = query / jnp.sqrt(jnp.sum(query * query, axis=0, keepdims=True) + EPS)
-        key = key / jnp.sqrt(jnp.sum(key * key, axis=0, keepdims=True) + EPS)
-        rows = []
-        for j in range(JW):
-            decayed = retain * mem[j]
-            recalled = jnp.sum(key * decayed, axis=0, keepdims=True)
-            updated = decayed + key * (strength * (value[j : j + 1] - recalled))
-            mem[j] = updated
-            rows.append(jnp.sum(query * updated, axis=0, keepdims=True) * DK**-0.5)
-        lead, rest = halves(jnp.concatenate(rows, axis=0))
-        readouts.append(contract(place, lead, 1, 1) + contract(place, rest, 1, 1))
+        ready[t, 0] = query / jnp.sqrt(jnp.sum(query * query, axis=0, keepdims=True) + EPS)
+        ready[t, 1] = key / jnp.sqrt(jnp.sum(key * key, axis=0, keepdims=True) + EPS)
+        ready[t, 2] = retain
+        rows8[t] = jnp.concatenate([value, jnp.broadcast_to(strength, (JW, SLOTS))], axis=0)
     kept = []
     for n in range(HIST):
         for part in range(3):
@@ -218,9 +210,25 @@
                 block = xt[mine, :]
             kept.append(block)
     kept = jnp.concatenate(kept, axis=0).astype(BF16)
-    kept = contract(places[STEPS - 1], kept, 1, 1)
-    pad = jnp.zeros((SLOTS, DK - BLOCKS * JW), F32)
-    return jnp.concatenate([kept] + readouts + [pad], axis=1)
+    return contract(places[STEPS - 1], kept, 1, 1)
+
+
+def run_steps(ready, rows8, places, mem):
+    readouts = []
+    for t in range(STEPS):
+        query, key, retain = ready[t, 0], ready[t, 1], ready[t, 2]
+        strength = rows8[t, JW : JW + 1, :]
+        rows = []
+        for j in range(JW):
+            decayed = retain * mem[j]
+            recalled = jnp.sum(key * decayed, axis=0, keepdims=True)
+            updated = decayed + key * (strength * (rows8[t, j : j + 1, :] - recalled))
+            mem[j] = updated
+            rows.append(jnp.sum(query * updated, axis=0, keepdims=True) * DK**-0.5)
+        lead, rest = halves(jnp.concatenate(rows, axis=0))
+        place = places[t]
+        readouts.append(contract(place, lead, 1, 1) + contract(place, rest, 1, 1))
+    return readouts
 
 
 def leave_states(place, mem, f1, b1):
@@ -349,6 +357,8 @@
     f2,
     mem,
     places,
+    ready,
+    rows8,
     xt,
     fc,
     fg,
@@ -368,9 +378,12 @@
             barrier, inc=1, device_id={axis: peer}, device_id_type=pl.DeviceIdType.MESH
         )
 
-    peers_far_first(me, functools.partial(greet, "rep"))
-    for k in range(1, columns):
+    for k in (4, 3, 5, 2, 6, 1, 7):
+        greet("rep", (lax.rem(z + k, ZS) * XS + x) * CS + core)
+    for k in (4, 3, 5, 2, 6, 1, 7):
         greet("head", lax.rem(col + k, columns))
+    for k in range(1, XS * CS):
+        greet("rep", z * XS * CS + lax.rem(x * CS + core + k, XS * CS))
 
     loads = [
         pltpu.make_async_copy(src, dst, local.at[n])
@@ -396,7 +409,7 @@
     for load in loads[:4]:
         load.wait()
     pack_inputs(conv, proj, decay, rate, s2, f)
-    pl.semaphore_wait(barrier, GROUPS - 1 + columns - 1)
+    pl.semaphore_wait(barrier, ZS - 1 + XS * CS - 1 + columns - 1)
 
     keep = pltpu.make_async_copy(s2.at[head], r2.at[core, x, z], local.at[12])
     keep.start()
@@ -484,8 +497,6 @@
     arrived(ring[5], opposite, 1)
     for copy in keep:
         copy.wait()
-    from_all(r1, 6)
-    enter_states(r1, f1, mem)
     for copy in ring:
         copy.wait_send()
     done = remote("rep", me, r2.at[0], r2.at[0], sems, 10)
@@ -494,9 +505,13 @@
     for n in range(XS):
         widen_inputs(r2, f2, 1 - core, n, 0, ZS)
     from_all(r3, 5)
-
     cols = pl.ds(pl.multiple_of(head * DK, DK), DK)
-    returned = run_steps(jg, f2, r3, taps.at[:, :, cols], places, mem, xt)
+    kept = prepare_steps(jg, f2, r3, taps.at[:, :, cols], places, ready, rows8, xt)
+    from_all(r1, 6)
+    enter_states(r1, f1, mem)
+    readouts = run_steps(ready, rows8, places, mem)
+    pad = jnp.zeros((SLOTS, DK - BLOCKS * JW), F32)
+    returned = jnp.concatenate([kept] + readouts + [pad], axis=1)
     for s in range(2):
         b2[:, s, :] = returned[s * GROUPS : (s + 1) * GROUPS]
     keep = pltpu.make_async_copy(b2.at[mine], a2.at[mine], local.at[12])
@@ -630,6 +645,8 @@
             pltpu.VMEM((GROUPS * ROWS, DK), F32),
             pltpu.VMEM((JW, DK, SLOTS), F32),
             pltpu.VMEM((STEPS, SLOTS, SLOTS), BF16),
+            pltpu.VMEM((STEPS, 3, DK, SLOTS), F32),
+            pltpu.VMEM((STEPS, 2 * JW, SLOTS), F32),
             pltpu.VMEM((DK, SLOTS), F32),
             pltpu.VMEM(operands[1].shape, F32),
             pltpu.VMEM((16, HEADS * DK), F32),

time: 50.2 us -> 48.2 us (0.960)
  Pallas kernels: 49.4 us -> 47.4 us
    pallas_call x1, Pallas kernels: 47.4 us -> 45.5 us  [local(): pl.pallas_call(functools.partial(whole, columns), out_shape=landed, in_sp...]
where the time goes in v5:
time: 48.2 us; the launch traced here: 48 us
  Pallas kernels  47.4 us (98%)
  between operations  0.64 us (1%)
    pallas_call x1, Pallas kernels, local(): pl.pallas_call(functools.partial(whole, columns), out_shape=landed, in_sp...  45.5 us
    pallas_call x1, Pallas kernels, local(): pl.pallas_call(settle, out_shape=results, in_specs=[any_] * 3, out_specs=...  1.95 us

profile of v5, /device:TPU:1, one launch (start us, length us, event | category | flops | bytes accessed | tf_op | source)
XLA Modules:
  0.0 48.0 jit_solution(11224720478446423853)
XLA Ops:
  0.6 45.5 %kda_steps.1 = (bf16[64,16,128]{2,1,0:T(8,128)(2,1)}, bf16[8,16,384]{2,1,0:T(8,128)(2,1)}, bf16[3,3,2,512]{3,2,1,0:T(2,128)(2,1)}) custom-call(f32[2,4,128,128]{3,2,1,0:T(8,128)} %states_in.1, bf16[3,3,2,512]{3,2,1,0:T(2,128)(2,1)} %bitcast.10, bf16[6,3,2,512]{3,2,1,0:T(2,128)(2,1)} %bitcast.8, f32[3,4,512]{2,1,0:T(4,128)} %bitcast.9, ...), custom_call_target="tpu_custom_call" | custom-call | tf_op jit(solution)/shard_map/kda_steps/pallas_call | solution.py:625
  46.1 1.9 %settle.1 = (bf16[6,2,288]{2,1,0:T(2,128)(2,1)}, f32[2,4,128,128]{3,2,1,0:T(8,128)}, bf16[3,3,2,512]{3,2,1,0:T(2,128)(2,1)}) custom-call(bf16[64,16,128]{2,1,0:T(8,128)(2,1)} %get-tuple-element.9.a1_in, bf16[8,16,384]{2,1,0:T(8,128)(2,1)} %get-tuple-element.10.shares_in, bf16[3,3,2,512]{3,2,1,0:T(2,128)(2,1)} %get-tuple-element.11.conv_in), custom_call_target="tpu_custom_call" | custom-call | tf_op jit(solution)/shard_map/settle/pallas_call | solution.py:664

commit v6 on v5

--- a/solution.py
+++ b/solution.py
@@ -170,7 +170,9 @@
         x = jnp.concatenate([both(w * 4), both(w * 4 + 2)] + extra, axis=1)
         return contract(x.astype(BF16), at, 0, 0)
 
-    start = contract(lead3, eye, 0, 0)
+    turned = contract(jnp.concatenate([lead3, rest3], axis=1), eye, 0, 0)
+    start = turned[:DK]
+    turned = turned.astype(BF16)
     hist = []
     for w in range(HIST):
         two = pair(w, [], eye)
@@ -178,7 +180,8 @@
     for t in range(STEPS):
         place = places[t]
         three = pair(t + HIST, [both(ROW_DECAY + 2 * t)], place)
-        small = contract(lead3, place, 0, 0) + contract(rest3, place, 0, 0)
+        small = contract(turned, place, 1, 0)
+        small = small[:DK] + small[DK:]
         new = [three[:DK], three[DK : 2 * DK], small[(t + HIST) * JW : (t + HIST + 1) * JW]]
         alive = small[LANE_ALIVE + t : LANE_ALIVE + t + 1] > 0.5
         logit = small[LANE_BETA + t : LANE_BETA + t + 1]
@@ -244,16 +247,26 @@
     lax.fori_loop(0, GROUPS, one, 0)
 
 
-def finish_rows(a2, gate, gain, live, weight, conv, partial, fc, fg):
+def ready_finish(gate, gain, live, spread, own, gains):
+    own[...] = own_lanes()
+    square = (DK, DK)
+    for b in range(BLOCKS):
+        spread[b] = jnp.where(iota(square, 0) == b * JW + (iota(square, 1) & 7), 1.0, 0.0).astype(BF16)
+    second = iota((2 * HEADS, DK), 0) >> 2
+    for t in range(STEPS):
+        gates = sigmoid(jnp.concatenate(by_head(gate[t].astype(F32)), axis=0)) * gain[...]
+        gains[t] = jnp.where(live[0:1, t : t + 1] > second, gates, 0.0)
+
+
+def finish_rows(a2, gains, spread, own, weight, conv, partial, fc, fg):
     lead, rest = halves(jnp.concatenate([a2[:, s, :] for s in range(2)], axis=0))
-    wide = (DK, BLOCKS * DK)
-    source = ((iota(wide, 1) >> 7) << 3) + (iota(wide, 1) & 7)
-    spread = jnp.where(iota(wide, 0) == source, 1.0, 0.0).astype(BF16)
-    every = contract(lead, spread, 1, 0) + contract(rest, spread, 1, 0)
-    mask = own_lanes()
+    mask = own[...]
 
     def block(b):
-        picked = every[:, b * DK : (b + 1) * DK] * mask
+        picked = contract(lead, spread[b], 1, 0)
+        if b >= CONV:
+            picked = picked + contract(rest, spread[b], 1, 0)
+        picked = picked * mask
         rows = []
         for s in range(2):
             total = picked[s * GROUPS : s * GROUPS + ZS]
@@ -263,13 +276,10 @@
         return jnp.concatenate(rows, axis=0)
 
     fg[...] = jnp.zeros_like(fg)
-    second = iota((2 * HEADS, DK), 0) >> 2
     for t in range(STEPS):
         readout = block(CONV + t)
         scaling = lax.rsqrt(jnp.sum(readout * readout, axis=1, keepdims=True) / DK + EPS)
-        gates = sigmoid(jnp.concatenate(by_head(gate[t].astype(F32)), axis=0))
-        gated = readout * scaling * gain[...] * gates
-        gated = jnp.where(live[0:1, t : t + 1] > second, gated, 0.0)
+        gated = readout * scaling * gains[t]
         for s in range(2):
             for h in range(HEADS):
                 r = s * HEADS + h
@@ -301,15 +311,28 @@
     )
 
 
-def peers_far_first(me, act):
-    act(lax.rem(me + GROUPS // 2, GROUPS))
-
-    def two(i, _):
-        act(lax.rem(me + 31 - i, GROUPS))
-        act(lax.rem(me + GROUPS - 31 + i, GROUPS))
-        return 0
-
-    lax.fori_loop(0, GROUPS // 2 - 1, two, 0)
+def peers_in_order(z, x, core, act, near=True, far=True):
+    def off(dz, dx, dc):
+        act(lax.rem(z + dz, ZS), lax.rem(x + dx, XS), lax.rem(core + dc, CS))
+
+    def along_z(dx, dc):
+        def one(q, _):
+            off(4 + (1 - 2 * (q % 2)) * ((q + 1) // 2), dx, dc)
+            return 0
+
+        lax.fori_loop(0, ZS - 1, one, 0)
+
+    if far:
+        for dx in (2, 1, 3):
+            for dc in (1, 0):
+                along_z(dx, dc)
+        along_z(0, 1)
+    if near:
+        along_z(0, 0)
+        for dx in (2, 1, 3):
+            off(0, dx, 1)
+            off(0, dx, 0)
+        off(0, 0, 1)
 
 
 def whole(
@@ -362,6 +385,9 @@
     xt,
     fc,
     fg,
+    spread,
+    own,
+    gains,
     local,
     sems,
 ):
@@ -418,10 +444,35 @@
         peer = (to * XS + x) * CS + core
         remote("rep", peer, s2.at[lax.rem(to, HEADS)], r2.at[core, x, z], sems, 0).start()
 
-    for load in loads[4:7]:
+    for load in loads[4:9]:
         load.wait()
     pack_values(conv, proj, beta, live, s3)
     pack_states(states, s1)
+    find_places(targets, places)
+
+    keep_s = [
+        pltpu.make_async_copy(s1.at[mine], r1.at[mine], local.at[13]),
+        pltpu.make_async_copy(s3.at[mine], r3.at[mine], local.at[14]),
+    ]
+    for copy in keep_s:
+        copy.start()
+
+    def to_all(pairs, **which):
+        def one(to_z, to_x, to_core):
+            at = (to_core * XS + to_x) * ZS + to_z
+            peer = (to_z * XS + to_x) * CS + to_core
+            for src, dst, n in pairs:
+                remote("rep", peer, src.at[at], dst.at[mine], sems, n).start()
+
+        peers_in_order(z, x, core, one, **which)
+
+    def from_all(dst, n):
+        most = dst.at[pl.ds(0, GROUPS - 1)]
+        done = remote("rep", me, most, most, sems, n)
+        done.wait_send()
+        done.wait_recv()
+
+    to_all([(s3, r3, 5), (s1, r1, 6)], far=False)
 
     keep.wait()
     done = remote("rep", me, r2.at[0, 0, pl.ds(0, ZS - 1)], r2.at[0, 0, pl.ds(0, ZS - 1)], sems, 0)
@@ -449,28 +500,7 @@
     ]
     remote("rep", other, r2.at[core, x], r2.at[core, x], sems, 10).start()
 
-    keep = [
-        pltpu.make_async_copy(s1.at[mine], r1.at[mine], local.at[13]),
-        pltpu.make_async_copy(s3.at[mine], r3.at[mine], local.at[14]),
-    ]
-    for copy in keep:
-        copy.start()
-
-    def to_all(pairs):
-        def one(p):
-            at = ((p % CS) * XS + (p // CS) % XS) * ZS + p // (XS * CS)
-            for src, dst, n in pairs:
-                remote("rep", p, src.at[at], dst.at[mine], sems, n).start()
-
-        peers_far_first(me, one)
-
-    def from_all(dst, n):
-        most = dst.at[pl.ds(0, GROUPS - 1)]
-        done = remote("rep", me, most, most, sems, n)
-        done.wait_send()
-        done.wait_recv()
-
-    to_all([(s3, r3, 5), (s1, r1, 6)])
+    to_all([(s3, r3, 5), (s1, r1, 6)], near=False)
 
     widen_inputs(r2, f2, core, x, 0, ZS)
 
@@ -485,9 +515,6 @@
     ring[1].wait_recv()
     ring.append(pass_on(left, ahead, 1, 12))
     pass_on(other, ahead, 1, 10)
-    for load in loads[7:9]:
-        load.wait()
-    find_places(targets, places)
     widen_inputs(r2, f2, core, behind, 0, half)
     widen_inputs(r2, f2, core, ahead, half, ZS)
     arrived(ring[2], behind, 1)
@@ -495,7 +522,7 @@
     opposite = lax.rem(x + 2, XS)
     arrived(ring[4], opposite, 0)
     arrived(ring[5], opposite, 1)
-    for copy in keep:
+    for copy in keep_s:
         copy.wait()
     for copy in ring:
         copy.wait_send()
@@ -521,12 +548,13 @@
     keep_states = pltpu.make_async_copy(b1.at[mine], a1.at[mine], local.at[13])
     keep_states.start()
     to_all([(b1, a1, 8)])
-
     for load in loads[9:]:
         load.wait()
+    ready_finish(gate, gain, live, spread, own, gains)
+
     keep.wait()
     from_all(a2, 7)
-    finish_rows(a2, gate, gain, live, weight, conv_out, partial, fc, fg)
+    finish_rows(a2, gains, spread, own, weight, conv_out, partial, fc, fg)
     keep = pltpu.make_async_copy(partial.at[col], shares.at[col], local.at[12])
     keep.start()
     for k in (4, 3, 5, 2, 6, 1, 7):
@@ -641,8 +669,8 @@
             small,
             pltpu.VMEM((columns, 16, width), BF16),
             pltpu.VMEM((HEADS, ROWS, DK), F32),
-            pltpu.VMEM((GROUPS * 16, DK), F32),
-            pltpu.VMEM((GROUPS * ROWS, DK), F32),
+            pltpu.VMEM(((GROUPS + 1) * 16, DK), F32),
+            pltpu.VMEM(((GROUPS + 1) * ROWS, DK), F32),
             pltpu.VMEM((JW, DK, SLOTS), F32),
             pltpu.VMEM((STEPS, SLOTS, SLOTS), BF16),
             pltpu.VMEM((STEPS, 3, DK, SLOTS), F32),
@@ -650,6 +678,9 @@
             pltpu.VMEM((DK, SLOTS), F32),
             pltpu.VMEM(operands[1].shape, F32),
             pltpu.VMEM((16, HEADS * DK), F32),
+            pltpu.VMEM((BLOCKS, DK, DK), BF16),
+            pltpu.VMEM((SLOTS, DK), F32),
+            pltpu.VMEM((STEPS, 2 * HEADS, DK), F32),
             pltpu.SemaphoreType.DMA((15,)),
             pltpu.SemaphoreType.DMA((2, 13)),
         ],

time: 48.2 us -> 47.5 us (0.985)
  Pallas kernels: 47.4 us -> 46.7 us
    pallas_call x1, Pallas kernels: 45.5 us -> 44.7 us  [local(): pl.pallas_call(functools.partial(whole, columns), out_shape=landed, in_sp...]
where the time goes in v6:
time: 47.5 us; the launch traced here: 47.3 us
  Pallas kernels  46.7 us (98%)
  between operations  0.64 us (1%)
    pallas_call x1, Pallas kernels, local(): pl.pallas_call(functools.partial(whole, columns), out_shape=landed, in_sp...  44.7 us
    pallas_call x1, Pallas kernels, local(): pl.pallas_call(settle, out_shape=results, in_specs=[any_] * 3, out_specs=...  1.95 us

profile of v6, /device:TPU:1, one launch (start us, length us, event | category | flops | bytes accessed | tf_op | source)
XLA Modules:
  0.0 47.3 jit_solution(15539593295637608598)
XLA Ops:
  0.6 44.7 %kda_steps.1 = (bf16[64,16,128]{2,1,0:T(8,128)(2,1)}, bf16[8,16,384]{2,1,0:T(8,128)(2,1)}, bf16[3,3,2,512]{3,2,1,0:T(2,128)(2,1)}) custom-call(f32[2,4,128,128]{3,2,1,0:T(8,128)} %states_in.1, bf16[3,3,2,512]{3,2,1,0:T(2,128)(2,1)} %bitcast.10, bf16[6,3,2,512]{3,2,1,0:T(2,128)(2,1)} %bitcast.8, f32[3,4,512]{2,1,0:T(4,128)} %bitcast.9, ...), custom_call_target="tpu_custom_call" | custom-call | tf_op jit(solution)/shard_map/kda_steps/pallas_call | solution.py:653
  45.4 1.9 %settle.1 = (bf16[6,2,288]{2,1,0:T(2,128)(2,1)}, f32[2,4,128,128]{3,2,1,0:T(8,128)}, bf16[3,3,2,512]{3,2,1,0:T(2,128)(2,1)}) custom-call(bf16[64,16,128]{2,1,0:T(8,128)(2,1)} %get-tuple-element.9.a1_in, bf16[8,16,384]{2,1,0:T(8,128)(2,1)} %get-tuple-element.10.shares_in, bf16[3,3,2,512]{3,2,1,0:T(2,128)(2,1)} %get-tuple-element.11.conv_in), custom_call_target="tpu_custom_call" | custom-call | tf_op jit(solution)/shard_map/settle/pallas_call | solution.py:695

commit v7 on v6

--- a/solution.py
+++ b/solution.py
@@ -119,13 +119,13 @@
             s1[holder(h, jg)] = jnp.concatenate([first[rows], second[rows]], axis=0).astype(BF16)
 
 
-def widen_inputs(r2, f2, core, x, first, last):
+def widen_inputs(r2, f2, core, x):
     def one(i, _):
         at = pl.multiple_of(((core * XS + x) * ZS + i) * ROWS, ROWS)
         f2[pl.ds(at, ROWS), :] = r2[core, x, i].astype(F32)
         return 0
 
-    lax.fori_loop(first, last, one, 0)
+    lax.fori_loop(0, ZS, one, 0)
 
 
 def enter_states(r1, f1, mem):
@@ -288,8 +288,11 @@
     width = partial.shape[2]
     share = total.shape[1] // partial.shape[0]
     for d in range(partial.shape[0]):
-        turned = total if d == 0 else pltpu.roll(total, total.shape[1] - d * share, 1)
-        partial[d] = turned[:, :width].astype(BF16)
+        base = d * share // DK * DK
+        piece = total[:, base : min(base + width + DK, total.shape[1])]
+        if d * share > base:
+            piece = pltpu.roll(piece, piece.shape[1] - (d * share - base), 1)
+        partial[d] = piece[:, :width].astype(BF16)
     for n in range(HIST):
         for part in range(3):
             kept = block(n * 3 + part)
@@ -481,47 +484,27 @@
     right = (z * XS + lax.rem(x + 1, XS)) * CS + core
     left = (z * XS + lax.rem(x + XS - 1, XS)) * CS + core
     other = me + 1 - 2 * core
-    half = ZS // 2
     behind, ahead = lax.rem(x + XS - 1, XS), lax.rem(x + 1, XS)
 
-    def part(origin, n):
-        return r2.at[core, origin, pl.ds(n * half, half)]
-
-    def pass_on(peer, origin, n, sem):
-        copy = remote("rep", peer, part(origin, n), part(origin, n), sems, sem)
+    opposite = lax.rem(x + 2, XS)
+    facing = (z * XS + opposite) * CS + core
+
+    def block_to(peer, origin, sem):
+        copy = remote("rep", peer, r2.at[core, origin], r2.at[core, origin], sems, sem)
         copy.start()
         return copy
 
-    ring = [
-        pass_on(right, x, 0, 1),
-        pass_on(left, x, 1, 2),
-        pass_on(right, x, 1, 3),
-        pass_on(left, x, 0, 4),
-    ]
-    remote("rep", other, r2.at[core, x], r2.at[core, x], sems, 10).start()
+    ring = [block_to(facing, x, 1), block_to(right, x, 2), block_to(left, x, 3)]
 
     to_all([(s3, r3, 5), (s1, r1, 6)], near=False)
 
-    widen_inputs(r2, f2, core, x, 0, ZS)
-
-    def arrived(copy, origin, n):
+    block_to(other, x, 10)
+    widen_inputs(r2, f2, core, x)
+
+    for copy, origin in ((ring[1], behind), (ring[2], ahead), (ring[0], opposite)):
         copy.wait_recv()
-        pass_on(other, origin, n, 10)
-        widen_inputs(r2, f2, core, origin, n * half, (n + 1) * half)
-
-    ring[0].wait_recv()
-    ring.append(pass_on(right, behind, 0, 11))
-    pass_on(other, behind, 0, 10)
-    ring[1].wait_recv()
-    ring.append(pass_on(left, ahead, 1, 12))
-    pass_on(other, ahead, 1, 10)
-    widen_inputs(r2, f2, core, behind, 0, half)
-    widen_inputs(r2, f2, core, ahead, half, ZS)
-    arrived(ring[2], behind, 1)
-    arrived(ring[3], ahead, 0)
-    opposite = lax.rem(x + 2, XS)
-    arrived(ring[4], opposite, 0)
-    arrived(ring[5], opposite, 1)
+        block_to(other, origin, 10)
+        widen_inputs(r2, f2, core, origin)
     for copy in keep_s:
         copy.wait()
     for copy in ring:
@@ -530,7 +513,7 @@
     done.wait_send()
     done.wait_recv()
     for n in range(XS):
-        widen_inputs(r2, f2, 1 - core, n, 0, ZS)
+        widen_inputs(r2, f2, 1 - core, n)
     from_all(r3, 5)
     cols = pl.ds(pl.multiple_of(head * DK, DK), DK)
     kept = prepare_steps(jg, f2, r3, taps.at[:, :, cols], places, ready, rows8, xt)
@@ -577,11 +560,19 @@
         pltpu.make_async_copy(src, dst, sems.at[n])
         for n, (src, dst) in enumerate([(a1_in, a1), (shares_in, shares), (conv_in, conv)])
     ]
-    for load in loads:
-        load.start()
+    for n in (1, 0, 2):
+        loads[n].start()
     loads[2].wait()
     stores = [pltpu.make_async_copy(conv, conv_to, sems.at[3])]
     stores[0].start()
+    loads[1].wait()
+    total = shares[0].astype(F32)
+    for n in range(1, shares.shape[0]):
+        total = total + shares[n].astype(F32)
+    for t in range(STEPS):
+        out[t] = total[2 * t : 2 * t + 2, : out.shape[2]].astype(BF16)
+    stores.append(pltpu.make_async_copy(out, out_to, sems.at[4 + 2 * HEADS]))
+    stores[-1].start()
     loads[0].wait()
     for h in range(HEADS):
         pieces = [a1[holder(h, jg)].astype(F32) for jg in range(JG)]
@@ -592,14 +583,6 @@
             )
             store.start()
             stores.append(store)
-    loads[1].wait()
-    total = shares[0].astype(F32)
-    for n in range(1, shares.shape[0]):
-        total = total + shares[n].astype(F32)
-    for t in range(STEPS):
-        out[t] = total[2 * t : 2 * t + 2, : out.shape[2]].astype(BF16)
-    stores.append(pltpu.make_async_copy(out, out_to, sems.at[4 + 2 * HEADS]))
-    stores[-1].start()
     for store in stores:
         store.wait()
 

time: 47.5 us -> 47.6 us (level)
  no operation moved by 1% of the time
where the time goes in v7:
time: 47.6 us; the launch traced here: 47.5 us
  Pallas kernels  46.8 us (98%)
  between operations  0.64 us (1%)
    pallas_call x1, Pallas kernels, local(): pl.pallas_call(functools.partial(whole, columns), out_shape=landed, in_sp...  44.8 us
    pallas_call x1, Pallas kernels, local(): pl.pallas_call(settle, out_shape=results, in_specs=[any_] * 3, out_specs=...  2 us

profile of v7, /device:TPU:1, one launch (start us, length us, event | category | flops | bytes accessed | tf_op | source)
XLA Modules:
  0.0 47.5 jit_solution(11143896272124697685)
XLA Ops:
  0.6 44.8 %kda_steps.1 = (bf16[64,16,128]{2,1,0:T(8,128)(2,1)}, bf16[8,16,384]{2,1,0:T(8,128)(2,1)}, bf16[3,3,2,512]{3,2,1,0:T(2,128)(2,1)}) custom-call(f32[2,4,128,128]{3,2,1,0:T(8,128)} %states_in.1, bf16[3,3,2,512]{3,2,1,0:T(2,128)(2,1)} %bitcast.10, bf16[6,3,2,512]{3,2,1,0:T(2,128)(2,1)} %bitcast.8, f32[3,4,512]{2,1,0:T(4,128)} %bitcast.9, ...), custom_call_target="tpu_custom_call" | custom-call | tf_op jit(solution)/shard_map/kda_steps/pallas_call | solution.py:636
  45.5 2.0 %settle.1 = (bf16[6,2,288]{2,1,0:T(2,128)(2,1)}, f32[2,4,128,128]{3,2,1,0:T(8,128)}, bf16[3,3,2,512]{3,2,1,0:T(2,128)(2,1)}) custom-call(bf16[64,16,128]{2,1,0:T(8,128)(2,1)} %get-tuple-element.9.a1_in, bf16[8,16,384]{2,1,0:T(8,128)(2,1)} %get-tuple-element.10.shares_in, bf16[3,3,2,512]{3,2,1,0:T(2,128)(2,1)} %get-tuple-element.11.conv_in), custom_call_target="tpu_custom_call" | custom-call | tf_op jit(solution)/shard_map/settle/pallas_call | solution.py:678

commit v8 on v6

--- a/solution.py
+++ b/solution.py
@@ -498,10 +498,11 @@
         pass_on(right, x, 1, 3),
         pass_on(left, x, 0, 4),
     ]
-    remote("rep", other, r2.at[core, x], r2.at[core, x], sems, 10).start()
 
     to_all([(s3, r3, 5), (s1, r1, 6)], near=False)
 
+    pass_whole = remote("rep", other, r2.at[core, x], r2.at[core, x], sems, 10)
+    pass_whole.start()
     widen_inputs(r2, f2, core, x, 0, ZS)
 
     def arrived(copy, origin, n):

time: 47.5 us -> 47.4 us (level)
  no operation moved by 1% of the time
where the time goes in v8:
time: 47.4 us; the launch traced here: 47.3 us
  Pallas kernels  46.6 us (98%)
  between operations  0.64 us (1%)
    pallas_call x1, Pallas kernels, local(): pl.pallas_call(functools.partial(whole, columns), out_shape=landed, in_sp...  44.7 us
    pallas_call x1, Pallas kernels, local(): pl.pallas_call(settle, out_shape=results, in_specs=[any_] * 3, out_specs=...  1.95 us

profile of v8, /device:TPU:1, one launch (start us, length us, event | category | flops | bytes accessed | tf_op | source)
XLA Modules:
  0.0 47.3 jit_solution(6300738125207275237)
XLA Ops:
  0.6 44.7 %kda_steps.1 = (bf16[64,16,128]{2,1,0:T(8,128)(2,1)}, bf16[8,16,384]{2,1,0:T(8,128)(2,1)}, bf16[3,3,2,512]{3,2,1,0:T(2,128)(2,1)}) custom-call(f32[2,4,128,128]{3,2,1,0:T(8,128)} %states_in.1, bf16[3,3,2,512]{3,2,1,0:T(2,128)(2,1)} %bitcast.10, bf16[6,3,2,512]{3,2,1,0:T(2,128)(2,1)} %bitcast.8, f32[3,4,512]{2,1,0:T(4,128)} %bitcast.9, ...), custom_call_target="tpu_custom_call" | custom-call | tf_op jit(solution)/shard_map/kda_steps/pallas_call | solution.py:654
  45.3 1.9 %settle.1 = (bf16[6,2,288]{2,1,0:T(2,128)(2,1)}, f32[2,4,128,128]{3,2,1,0:T(8,128)}, bf16[3,3,2,512]{3,2,1,0:T(2,128)(2,1)}) custom-call(bf16[64,16,128]{2,1,0:T(8,128)(2,1)} %get-tuple-element.9.a1_in, bf16[8,16,384]{2,1,0:T(8,128)(2,1)} %get-tuple-element.10.shares_in, bf16[3,3,2,512]{3,2,1,0:T(2,128)(2,1)} %get-tuple-element.11.conv_in), custom_call_target="tpu_custom_call" | custom-call | tf_op jit(solution)/shard_map/settle/pallas_call | solution.py:696
